TPU v7x, 32 devices: a whole 2x2x4 slice. The times are simulated.
32 devices in a mesh: sec: 16 (over z, y, x), blk: 2 (over core).
Axes of the slice: x: 2, y: 2, z: 4, core: 2. Of those that a mesh axis runs over, the one named last changes fastest.
Arguments:
- slab_state: float32 [9, 8, 256, 256], P(None, None, 'sec', 'blk'), may hold values from -6 to 6
- buoyancy: float32 [8, 256, 256], P(None, 'sec', 'blk'), may hold values from 0.5 to 1
- lame_lambda: float32 [8, 256, 256], P(None, 'sec', 'blk'), may hold values from 0.5 to 2
- lame_mu: float32 [8, 256, 256], P(None, 'sec', 'blk'), may hold values from 0.3 to 1.2
- face_map: int32 [256], replicated, may hold values from 0 to 1023
- band_widths: int32 [16, 2], P('sec'), may hold values from 2 to 9
- ocean_state: float32 [3, 256, 1024], P(None, 'sec', 'blk'), may hold values from -6 to 6
- water_depth: float32 [256, 1024], P('sec', 'blk'), may hold values from 0.25 to 1
Outputs:
- slab_out: float32 [9, 8, 256, 256], P(None, None, 'sec', 'blk')
- ocean_out: float32 [3, 256, 1024], P(None, 'sec', 'blk')
Inputs may be any that keep to these rules, and one draw needn't show every extreme that they name: `face_map`: each entry is the ocean column over which that seafloor face column lies. `band_widths`: the Kajiura band width of each ocean tile in ocean cells.
All inputs are finite; a program needn't handle non-finite values.
Results may differ from a plain program's by a relative error of at most 0.00014.
Values sent between devices are 32-bit elements; how exact they have to be, the bound alone decides.
A program may use at most 64 MiB of HBM per device.

v0:
```python
import math

import jax
import jax.numpy as jnp
from jax import lax
from jax.sharding import PartitionSpec as P

SLAB_STEPS = 2
WAVE_STEPS = 4


time_step = 0.25
wave_step = 0.5


def padded(x, sides, width):
    for axis, dim in sides:
        devices, length = (lax.axis_size(axis), x.shape[dim])
        up = [(i, (i + 1) % devices) for i in range(devices - 1)]
        down = [(j, i) for i, j in up]
        last = lax.slice_in_dim(x, length - width, length, axis=dim)
        leading = lax.slice_in_dim(x, 0, width, axis=dim)
        before = lax.ppermute(last, axis, up)
        after = lax.ppermute(leading, axis, down)
        x = jnp.concatenate([before, x, after], axis=dim)
    return x


def sech_kernel(distance, band_width):
    scaled = jnp.abs(distance) * (math.pi / 2.0) / band_width
    decay = jnp.exp(-scaled)
    return 2.0 * decay / (1.0 + decay * decay) / (2.0 * band_width)


def offset_slice(values, dimension, offset):
    slicer = [slice(1, -1)] * 3
    extent = values.shape[dimension]
    slicer[dimension] = slice(1 + offset, extent - 1 + offset)
    return values[tuple(slicer)]


def forward(values, dimension):
    return offset_slice(values, dimension, 1) - offset_slice(values, dimension, 0)


def backward(values, dimension):
    return offset_slice(values, dimension, 0) - offset_slice(values, dimension, -1)


def new_velocity(velocity, stress_padded, buoyancy):
    results = []
    for dimension in range(3):
        summed = forward(stress_padded[dimension], dimension)
        for across in range(3):
            if across != dimension:
                summed = summed + backward(stress_padded[6 - dimension - across], across)
        results.append(velocity[dimension] + time_step * buoyancy * summed)
    return jnp.stack(results)


def new_stress(stress, velocity_padded, lame_lambda, lame_mu):
    strain_rates = [backward(velocity_padded[dimension], dimension) for dimension in range(3)]
    dilatation = strain_rates[0] + strain_rates[1] + strain_rates[2]
    results = []
    for dimension in range(3):
        results.append(
            stress[dimension]
            + time_step * (lame_lambda * dilatation + 2.0 * lame_mu * strain_rates[dimension])
        )
    results.append(
        stress[3]
        + time_step * lame_mu * (forward(velocity_padded[1], 2) + forward(velocity_padded[2], 1))
    )
    results.append(
        stress[4]
        + time_step * lame_mu * (forward(velocity_padded[0], 2) + forward(velocity_padded[2], 0))
    )
    results.append(
        stress[5]
        + time_step * lame_mu * (forward(velocity_padded[0], 1) + forward(velocity_padded[1], 0))
    )
    return jnp.stack(results)


def pad_thickness(values):
    return jnp.pad(values, ((0, 0), (1, 1), (0, 0), (0, 0)))


def domain_mask(row_index, row_count, row_extent, col_index, col_count, col_extent, margin):
    row_cells = (
        row_index * row_extent - margin + jnp.arange(row_extent + 2 * margin, dtype=jnp.int32)
    )
    col_cells = (
        col_index * col_extent - margin + jnp.arange(col_extent + 2 * margin, dtype=jnp.int32)
    )
    row_valid = (row_cells >= 0) & (row_cells < row_count * row_extent)
    col_valid = (col_cells >= 0) & (col_cells < col_count * col_extent)
    return (row_valid[:, None] & col_valid[None, :]).astype(jnp.float32)


def on_device(
    slab_state, buoyancy, lame_lambda, lame_mu, face_map, band_widths, ocean_state, water_depth
):
    strike_dev = slab_state.shape[2]
    dip_dev = slab_state.shape[3]
    ocean_dev = ocean_state.shape[2]
    sec_index = lax.axis_index("sec")
    blk_index = lax.axis_index("blk")
    sec_count = lax.axis_size("sec")
    blk_count = lax.axis_size("blk")
    surface_rate = jnp.zeros((strike_dev, dip_dev), jnp.float32)
    velocity = slab_state[:3]
    stress = slab_state[3:]
    for stepping in range(SLAB_STEPS):
        stress_wide = padded(stress, (("sec", 2), ("blk", 3)), 1)
        velocity = new_velocity(velocity, pad_thickness(stress_wide), buoyancy)
        surface_rate = surface_rate + velocity[0, 0]
        velocity_wide = padded(velocity, (("sec", 2), ("blk", 3)), 1)
        stress = new_stress(stress, pad_thickness(velocity_wide), lame_lambda, lame_mu)
    slab_out = jnp.concatenate([velocity, stress], 0)
    uplift = time_step * surface_rate
    own_map = lax.dynamic_slice_in_dim(face_map, blk_index * dip_dev, dip_dev, 0)
    widths = jnp.repeat(band_widths[0], ocean_dev).astype(jnp.float32)
    columns = jnp.arange(ocean_dev * blk_count, dtype=jnp.int32)
    distance = (columns[:, None] - own_map[None, :]).astype(jnp.float32)
    kernel = sech_kernel(distance, widths[:, None])
    partial_value = jnp.einsum("xy,cy->xc", uplift, kernel, precision=lax.Precision.HIGHEST)
    source = lax.psum_scatter(partial_value, "blk", scatter_dimension=1, tiled=True)
    fields = jnp.stack([ocean_state[0] + source, ocean_state[1], ocean_state[2]])
    wet_mask = domain_mask(sec_index, sec_count, strike_dev, blk_index, blk_count, ocean_dev, 1)
    for stepping in range(WAVE_STEPS):
        extended_ocean = padded(fields, (("sec", 1), ("blk", 2)), 2)
        level = extended_ocean[0]
        flux_strike = extended_ocean[1]
        flux_dip = extended_ocean[2]
        surface = (
            level[1:-1, 1:-1]
            - wave_step
            * 0.5
            * (
                flux_strike[2:, 1:-1]
                - flux_strike[:-2, 1:-1]
                + (flux_dip[1:-1, 2:] - flux_dip[1:-1, :-2])
            )
        ) * wet_mask
        new_strike = flux_strike[2:-2, 2:-2] - wave_step * 0.5 * water_depth * (
            surface[2:, 1:-1] - surface[:-2, 1:-1]
        )
        new_dip = flux_dip[2:-2, 2:-2] - wave_step * 0.5 * water_depth * (
            surface[1:-1, 2:] - surface[1:-1, :-2]
        )
        fields = jnp.stack([surface[1:-1, 1:-1], new_strike, new_dip])
    return (slab_out, fields)


def solution(mesh):
    in_specs = (
        P(None, None, "sec", "blk"),
        P(None, "sec", "blk"),
        P(None, "sec", "blk"),
        P(None, "sec", "blk"),
        P(),
        P("sec", None),
        P(None, "sec", "blk"),
        P("sec", "blk"),
    )
    out_specs = (P(None, None, "sec", "blk"), P(None, "sec", "blk"))
    return jax.shard_map(
        on_device, mesh=mesh, in_specs=in_specs, out_specs=out_specs, check_vma=False
    )
```

profile of v0, /device:TPU:8, one launch (start us, length us, event | category | flops | bytes accessed | tf_op | source)
XLA Modules:
  0.0 142.5 jit_solution(6791492516167510799)
XLA Ops:
  7.2 1.1 fusion.111
  8.3 3.4 %collective-permute-start = (f32[6,8,1,128]{3,1,2,0:T(8,128)S(1)}, f32[6,8,1,128]{3,1,2,0:T(8,128)S(1)}, u32[]{:S(2)}, u32[]{:S(2)}) collective-permute-start(f32[6,8,1,128]{3,1,2,0:T(8,128)S(1)} %bitcast.185), channel_id=1, source_target_pairs={{0,2},{2,4},{4,6},{6,8},{8,10},{10,12},{12,14},{14,16},{16,18},{18... | collective-permute-start | bytes 73736 | tf_op jit(solution)/shard_map/ppermute | solution.py:23
  11.7 4.2 %collective-permute-start.1 = (f32[6,8,1,128]{3,1,2,0:T(8,128)S(1)}, f32[6,8,1,128]{3,1,2,0:T(8,128)S(1)}, u32[]{:S(2)}, u32[]{:S(2)}) collective-permute-start(f32[6,8,1,128]{3,1,2,0:T(8,128)S(1)} %bitcast.184), channel_id=1, source_target_pairs={{2,0},{4,2},{6,4},{8,6},{10,8},{12,10},{14,12},{16,14},{18,16},{20... | collective-permute-start | bytes 73736 | tf_op jit(solution)/shard_map/ppermute | solution.py:24
  16.0 1.1 fusion.110
  18.1 1.3 collective-permute-start.2
  19.4 0.4 copy.122
  19.8 1.3 collective-permute-start.3
  21.1 0.4 copy.90
  21.5 1.4 collective-permute-done.3
  22.8 0.4 copy.91
  23.2 0.8 select_maximum_fusion.4
  24.3 0.6 copy-done.1
  25.3 4.3 %collective-permute-start.4 = (f32[3,8,1,128]{3,1,2,0:T(8,128)S(1)}, f32[3,8,1,128]{3,1,2,0:T(8,128)S(1)}, u32[]{:S(2)}, u32[]{:S(2)}) collective-permute-start(f32[3,8,1,128]{3,1,2,0:T(8,128)S(1)} %get-tuple-element.68), channel_id=1, source_target_pairs={{0,2},{2,4},{4,6},{6,8},{8,10},{10,12},{12,14},{14,16},{16,18},{18... | collective-permute-start | bytes 36872 | tf_op jit(solution)/shard_map/ppermute | solution.py:23
  29.6 3.7 %collective-permute-start.5 = (f32[3,8,1,128]{3,1,2,0:T(8,128)S(1)}, f32[3,8,1,128]{3,1,2,0:T(8,128)S(1)}, u32[]{:S(2)}, u32[]{:S(2)}) collective-permute-start(f32[3,8,1,128]{3,1,2,0:T(8,128)S(1)} %get-tuple-element.69), channel_id=1, source_target_pairs={{2,0},{4,2},{6,4},{8,6},{10,8},{12,10},{14,12},{16,14},{18,16},{20... | collective-permute-start | bytes 36872 | tf_op jit(solution)/shard_map/ppermute | solution.py:24
  33.3 1.8 %collective-permute-done.5 = f32[3,8,1,128]{3,1,2,0:T(8,128)S(1)} collective-permute-done((f32[3,8,1,128]{3,1,2,0:T(8,128)S(1)}, f32[3,8,1,128]{3,1,2,0:T(8,128)S(1)}, u32[]{:S(2)}, u32[]{:S(2)}) %collective-permute-start.5) | collective-permute-done | bytes 12320 | tf_op jit(solution)/shard_map/ppermute | solution.py:24
  35.3 1.4 %collective-permute-start.6 = (f32[3,8,18,1]{3,1,2,0:T(8,128)S(1)}, f32[3,8,18,1]{3,1,2,0:T(8,128)S(1)}, u32[]{:S(2)}, u32[]{:S(2)}) collective-permute-start(f32[3,8,18,1]{3,1,2,0:T(8,128)S(1)} %get-tuple-element.64), channel_id=1, source_target_pairs={{0,1},{2,3},{4,5},{6,7},{8,9},{10,11},{12,13},{14,15},{16,17},{18,... | collective-permute-start | bytes 5192 | tf_op jit(solution)/shard_map/ppermute | solution.py:23
  36.8 1.3 collective-permute-start.7
  38.1 2.0 %collective-permute-done.7 = f32[3,8,18,1]{3,1,2,0:T(8,128)S(1)} collective-permute-done((f32[3,8,18,1]{3,1,2,0:T(8,128)S(1)}, f32[3,8,18,1]{3,1,2,0:T(8,128)S(1)}, u32[]{:S(2)}, u32[]{:S(2)}) %collective-permute-start.7) | collective-permute-done | bytes 1760 | tf_op jit(solution)/shard_map/ppermute | solution.py:24
  40.2 0.5 select_maximum_fusion.12
  41.5 3.8 %collective-permute-start.8 = (f32[6,8,1,128]{3,1,2,0:T(8,128)S(1)}, f32[6,8,1,128]{3,1,2,0:T(8,128)S(1)}, u32[]{:S(2)}, u32[]{:S(2)}) collective-permute-start(f32[6,8,1,128]{3,1,2,0:T(8,128)S(1)} %get-tuple-element.54), channel_id=1, source_target_pairs={{0,2},{2,4},{4,6},{6,8},{8,10},{10,12},{12,14},{14,16},{16,18},{18... | collective-permute-start | bytes 73736 | tf_op jit(solution)/shard_map/ppermute | solution.py:23
  45.3 3.9 %collective-permute-start.9 = (f32[6,8,1,128]{3,1,2,0:T(8,128)S(1)}, f32[6,8,1,128]{3,1,2,0:T(8,128)S(1)}, u32[]{:S(2)}, u32[]{:S(2)}) collective-permute-start(f32[6,8,1,128]{3,1,2,0:T(8,128)S(1)} %get-tuple-element.55), channel_id=1, source_target_pairs={{2,0},{4,2},{6,4},{8,6},{10,8},{12,10},{14,12},{16,14},{18,16},{20... | collective-permute-start | bytes 73736 | tf_op jit(solution)/shard_map/ppermute | solution.py:24
  49.3 1.8 %collective-permute-done.9 = f32[6,8,1,128]{3,1,2,0:T(8,128)S(1)} collective-permute-done((f32[6,8,1,128]{3,1,2,0:T(8,128)S(1)}, f32[6,8,1,128]{3,1,2,0:T(8,128)S(1)}, u32[]{:S(2)}, u32[]{:S(2)}) %collective-permute-start.9) | collective-permute-done | bytes 24608 | tf_op jit(solution)/shard_map/ppermute | solution.py:24
  51.3 0.4 copy.103
  51.7 1.3 collective-permute-start.10
  53.0 0.4 copy.104
  53.3 1.3 collective-permute-start.11
  54.8 0.4 copy.105
  55.2 1.3 collective-permute-done.11
  56.4 0.4 copy.106
  56.8 0.8 select_maximum_fusion
  58.1 1.5 %fusion.2 = f32[16,1024]{1,0:T(8,128)} fusion(f32[16,128]{1,0:T(8,128)S(1)} %bitcast.188, f32[1024]{0:T(1024)S(1)} %broadcast_multiply_fusion, f32[1024]{0:T(1024)S(1)} %bitcast.187, s32[128]{0:T(128)S(1)} %dynamic_slice.3), kind=kOutput, calls=%fused_computation.25 | convolution fusion | flops 26607616 | bytes 82432 | tf_op jit(solution)/shard_map/xy,cy->xc/dot_general | solution.py:127
  59.8 4.8 %collective-permute-start.12 = (f32[3,8,1,128]{3,1,2,0:T(8,128)S(1)}, f32[3,8,1,128]{3,1,2,0:T(8,128)S(1)}, u32[]{:S(2)}, u32[]{:S(2)}) collective-permute-start(f32[3,8,1,128]{3,1,2,0:T(8,128)S(1)} %get-tuple-element.66), channel_id=1, source_target_pairs={{0,2},{2,4},{4,6},{6,8},{8,10},{10,12},{12,14},{14,16},{16,18},{18... | collective-permute-start | bytes 36872 | tf_op jit(solution)/shard_map/ppermute | solution.py:23
  64.6 2.8 %collective-permute-start.13 = (f32[3,8,1,128]{3,1,2,0:T(8,128)S(1)}, f32[3,8,1,128]{3,1,2,0:T(8,128)S(1)}, u32[]{:S(2)}, u32[]{:S(2)}) collective-permute-start(f32[3,8,1,128]{3,1,2,0:T(8,128)S(1)} %get-tuple-element.67), channel_id=1, source_target_pairs={{2,0},{4,2},{6,4},{8,6},{10,8},{12,10},{14,12},{16,14},{18,16},{20... | collective-permute-start | bytes 36872 | tf_op jit(solution)/shard_map/ppermute | solution.py:24
  67.5 2.7 %collective-permute-done.13 = f32[3,8,1,128]{3,1,2,0:T(8,128)S(1)} collective-permute-done((f32[3,8,1,128]{3,1,2,0:T(8,128)S(1)}, f32[3,8,1,128]{3,1,2,0:T(8,128)S(1)}, u32[]{:S(2)}, u32[]{:S(2)}) %collective-permute-start.13) | collective-permute-done | bytes 12320 | tf_op jit(solution)/shard_map/ppermute | solution.py:24
  70.4 1.3 collective-permute-start.14
  71.7 1.3 collective-permute-start.15
  73.0 2.0 %collective-permute-done.15 = f32[3,8,18,1]{3,1,2,0:T(8,128)S(1)} collective-permute-done((f32[3,8,18,1]{3,1,2,0:T(8,128)S(1)}, f32[3,8,18,1]{3,1,2,0:T(8,128)S(1)}, u32[]{:S(2)}, u32[]{:S(2)}) %collective-permute-start.15) | collective-permute-done | bytes 1760 | tf_op jit(solution)/shard_map/ppermute | solution.py:24
  75.0 0.5 select_maximum_fusion.6
  75.6 0.8 fusion.96
  76.4 3.7 %collective-permute-start.16 = (f32[3,2,512]{2,1,0:T(2,128)S(1)}, f32[3,2,512]{2,1,0:T(2,128)S(1)}, u32[]{:S(2)}, u32[]{:S(2)}) collective-permute-start(f32[3,2,512]{2,1,0:T(2,128)S(1)} %get-tuple-element.97), channel_id=1, source_target_pairs={{0,2},{2,4},{4,6},{6,8},{8,10},{10,12},{12,14},{14,16},{16,18},{18... | collective-permute-start | bytes 36872 | tf_op jit(solution)/shard_map/ppermute | solution.py:23
  80.1 3.9 %collective-permute-start.17 = (f32[3,2,512]{2,1,0:T(2,128)S(1)}, f32[3,2,512]{2,1,0:T(2,128)S(1)}, u32[]{:S(2)}, u32[]{:S(2)}) collective-permute-start(f32[3,2,512]{2,1,0:T(2,128)S(1)} %get-tuple-element.98), channel_id=1, source_target_pairs={{2,0},{4,2},{6,4},{8,6},{10,8},{12,10},{14,12},{16,14},{18,16},{20... | collective-permute-start | bytes 36872 | tf_op jit(solution)/shard_map/ppermute | solution.py:24
  84.3 1.4 collective-permute-done.17
  85.8 1.3 collective-permute-start.18
  87.1 1.3 collective-permute-start.19
  88.6 1.6 %collective-permute-done.19 = f32[3,20,2]{2,1,0:T(8,128)S(1)} collective-permute-done((f32[3,20,2]{2,1,0:T(8,128)S(1)}, f32[3,20,2]{2,1,0:T(8,128)S(1)}, u32[]{:S(2)}, u32[]{:S(2)}) %collective-permute-start.19) | collective-permute-done | bytes 512 | tf_op jit(solution)/shard_map/ppermute | solution.py:24
  90.7 4.0 %collective-permute-start.20 = (f32[3,2,512]{2,1,0:T(2,128)S(1)}, f32[3,2,512]{2,1,0:T(2,128)S(1)}, u32[]{:S(2)}, u32[]{:S(2)}) collective-permute-start(f32[3,2,512]{2,1,0:T(2,128)S(1)} %get-tuple-element.95), channel_id=1, source_target_pairs={{0,2},{2,4},{4,6},{6,8},{8,10},{10,12},{12,14},{14,16},{16,18},{18... | collective-permute-start | bytes 36872 | tf_op jit(solution)/shard_map/ppermute | solution.py:23
  94.7 3.7 %collective-permute-start.21 = (f32[3,2,512]{2,1,0:T(2,128)S(1)}, f32[3,2,512]{2,1,0:T(2,128)S(1)}, u32[]{:S(2)}, u32[]{:S(2)}) collective-permute-start(f32[3,2,512]{2,1,0:T(2,128)S(1)} %get-tuple-element.96), channel_id=1, source_target_pairs={{2,0},{4,2},{6,4},{8,6},{10,8},{12,10},{14,12},{16,14},{18,16},{20... | collective-permute-start | bytes 36872 | tf_op jit(solution)/shard_map/ppermute | solution.py:24
  98.4 1.9 %collective-permute-done.21 = f32[3,2,512]{2,1,0:T(2,128)S(1)} collective-permute-done((f32[3,2,512]{2,1,0:T(2,128)S(1)}, f32[3,2,512]{2,1,0:T(2,128)S(1)}, u32[]{:S(2)}, u32[]{:S(2)}) %collective-permute-start.21) | collective-permute-done | bytes 12320 | tf_op jit(solution)/shard_map/ppermute | solution.py:24
  100.3 1.3 collective-permute-start.22
  101.7 1.3 collective-permute-start.23
  103.0 1.8 %collective-permute-done.23 = f32[3,20,2]{2,1,0:T(8,128)S(1)} collective-permute-done((f32[3,20,2]{2,1,0:T(8,128)S(1)}, f32[3,20,2]{2,1,0:T(8,128)S(1)}, u32[]{:S(2)}, u32[]{:S(2)}) %collective-permute-start.23) | collective-permute-done | bytes 512 | tf_op jit(solution)/shard_map/ppermute | solution.py:24
  105.2 3.8 %collective-permute-start.24 = (f32[3,2,512]{2,1,0:T(2,128)S(1)}, f32[3,2,512]{2,1,0:T(2,128)S(1)}, u32[]{:S(2)}, u32[]{:S(2)}) collective-permute-start(f32[3,2,512]{2,1,0:T(2,128)S(1)} %get-tuple-element.93), channel_id=1, source_target_pairs={{0,2},{2,4},{4,6},{6,8},{8,10},{10,12},{12,14},{14,16},{16,18},{18... | collective-permute-start | bytes 36872 | tf_op jit(solution)/shard_map/ppermute | solution.py:23
  109.0 3.9 %collective-permute-start.25 = (f32[3,2,512]{2,1,0:T(2,128)S(1)}, f32[3,2,512]{2,1,0:T(2,128)S(1)}, u32[]{:S(2)}, u32[]{:S(2)}) collective-permute-start(f32[3,2,512]{2,1,0:T(2,128)S(1)} %get-tuple-element.94), channel_id=1, source_target_pairs={{2,0},{4,2},{6,4},{8,6},{10,8},{12,10},{14,12},{16,14},{18,16},{20... | collective-permute-start | bytes 36872 | tf_op jit(solution)/shard_map/ppermute | solution.py:24
  112.9 1.7 %collective-permute-done.25 = f32[3,2,512]{2,1,0:T(2,128)S(1)} collective-permute-done((f32[3,2,512]{2,1,0:T(2,128)S(1)}, f32[3,2,512]{2,1,0:T(2,128)S(1)}, u32[]{:S(2)}, u32[]{:S(2)}) %collective-permute-start.25) | collective-permute-done | bytes 12320 | tf_op jit(solution)/shard_map/ppermute | solution.py:24
  114.7 1.3 collective-permute-start.26
  116.0 1.3 collective-permute-start.27
  117.3 1.8 %collective-permute-done.27 = f32[3,20,2]{2,1,0:T(8,128)S(1)} collective-permute-done((f32[3,20,2]{2,1,0:T(8,128)S(1)}, f32[3,20,2]{2,1,0:T(8,128)S(1)}, u32[]{:S(2)}, u32[]{:S(2)}) %collective-permute-start.27) | collective-permute-done | bytes 512 | tf_op jit(solution)/shard_map/ppermute | solution.py:24
  119.6 4.8 %collective-permute-start.28 = (f32[3,2,512]{2,1,0:T(2,128)S(1)}, f32[3,2,512]{2,1,0:T(2,128)S(1)}, u32[]{:S(2)}, u32[]{:S(2)}) collective-permute-start(f32[3,2,512]{2,1,0:T(2,128)S(1)} %get-tuple-element.91), channel_id=1, source_target_pairs={{0,2},{2,4},{4,6},{6,8},{8,10},{10,12},{12,14},{14,16},{16,18},{18... | collective-permute-start | bytes 36872 | tf_op jit(solution)/shard_map/ppermute | solution.py:23
  124.4 2.8 %collective-permute-start.29 = (f32[3,2,512]{2,1,0:T(2,128)S(1)}, f32[3,2,512]{2,1,0:T(2,128)S(1)}, u32[]{:S(2)}, u32[]{:S(2)}) collective-permute-start(f32[3,2,512]{2,1,0:T(2,128)S(1)} %get-tuple-element.92), channel_id=1, source_target_pairs={{2,0},{4,2},{6,4},{8,6},{10,8},{12,10},{14,12},{16,14},{18,16},{20... | collective-permute-start | bytes 36872 | tf_op jit(solution)/shard_map/ppermute | solution.py:24
  127.3 2.7 %collective-permute-done.29 = f32[3,2,512]{2,1,0:T(2,128)S(1)} collective-permute-done((f32[3,2,512]{2,1,0:T(2,128)S(1)}, f32[3,2,512]{2,1,0:T(2,128)S(1)}, u32[]{:S(2)}, u32[]{:S(2)}) %collective-permute-start.29) | collective-permute-done | bytes 12320 | tf_op jit(solution)/shard_map/ppermute | solution.py:24
  130.1 1.3 collective-permute-start.30
  131.4 1.3 collective-permute-start.31
  132.7 1.8 %collective-permute-done.31 = f32[3,20,2]{2,1,0:T(8,128)S(1)} collective-permute-done((f32[3,20,2]{2,1,0:T(8,128)S(1)}, f32[3,20,2]{2,1,0:T(8,128)S(1)}, u32[]{:S(2)}, u32[]{:S(2)}) %collective-permute-start.31) | collective-permute-done | bytes 512 | tf_op jit(solution)/shard_map/ppermute | solution.py:24
  135.0 0.6 pad_maximum_fusion.7
  (109 shorter events, 6.5 us)
Async XLA Ops:
  7.2 10.0 %slice-start = ((f32[9,8,16,128]{3,2,1,0:T(8,128)}), f32[6,8,16,128]{3,2,1,0:T(8,128)S(1)}, s32[]{:S(2)}) async-start(f32[9,8,16,128]{3,2,1,0:T(8,128)} %param.8), calls=%async_computation.2 | async-start | bytes 786432 | tf_op jit(solution)/shard_map/slice | solution.py:113
  7.2 68.4 %reduce-scatter.2.cloned.1.call-start = ((), (), s32[]{:S(2)}) async-start(), calls=%async_computation.1 | async-start | bytes 98304 | tf_op jit(solution)/shard_map/reduce_scatter | solution.py:128
  8.3 8.8 %collective-permute-start = (f32[6,8,1,128]{3,1,2,0:T(8,128)S(1)}, f32[6,8,1,128]{3,1,2,0:T(8,128)S(1)}, u32[]{:S(2)}, u32[]{:S(2)}) collective-permute-start(f32[6,8,1,128]{3,1,2,0:T(8,128)S(1)} %bitcast.185), channel_id=1, source_target_pairs={{0,2},{2,4},{4,6},{6,8},{8,10},{10,12},{12,14},{14,16},{16,18},{18... | collective-permute-start | bytes 73736 | tf_op jit(solution)/shard_map/ppermute | solution.py:23
  11.7 5.7 %collective-permute-start.1 = (f32[6,8,1,128]{3,1,2,0:T(8,128)S(1)}, f32[6,8,1,128]{3,1,2,0:T(8,128)S(1)}, u32[]{:S(2)}, u32[]{:S(2)}) collective-permute-start(f32[6,8,1,128]{3,1,2,0:T(8,128)S(1)} %bitcast.184), channel_id=1, source_target_pairs={{2,0},{4,2},{6,4},{8,6},{10,8},{12,10},{14,12},{16,14},{18,16},{20... | collective-permute-start | bytes 73736 | tf_op jit(solution)/shard_map/ppermute | solution.py:24
  17.2 3.9 %copy-start.7 = (s32[1,2]{1,0:T(1,128)S(1)}, s32[1,2]{1,0:T(1,128)}, u32[]{:S(2)}) copy-start(s32[1,2]{1,0:T(1,128)} %param.13) | copy-start | bytes 28
  18.1 3.0 %collective-permute-start.2 = (f32[6,8,18,1]{2,1,3,0:T(8,128)S(1)}, f32[6,8,18,1]{2,1,3,0:T(8,128)S(1)}, u32[]{:S(2)}, u32[]{:S(2)}) collective-permute-start(f32[6,8,18,1]{2,1,3,0:T(8,128)S(1)} %copy.121), channel_id=1, source_target_pairs={{0,1},{2,3},{4,5},{6,7},{8,9},{10,11},{12,13},{14,15},{16,17},{18,... | collective-permute-start | bytes 10376 | tf_op jit(solution)/shard_map/ppermute | solution.py:23
  19.8 3.1 %collective-permute-start.3 = (f32[6,8,18,1]{2,1,3,0:T(8,128)S(1)}, f32[6,8,18,1]{2,1,3,0:T(8,128)S(1)}, u32[]{:S(2)}, u32[]{:S(2)}) collective-permute-start(f32[6,8,18,1]{2,1,3,0:T(8,128)S(1)} %copy.122), channel_id=1, source_target_pairs={{1,0},{3,2},{5,4},{7,6},{9,8},{11,10},{13,12},{15,14},{17,16},{19,... | collective-permute-start | bytes 10376 | tf_op jit(solution)/shard_map/ppermute | solution.py:24
  24.0 0.8 copy-start.1
  25.3 8.0 %collective-permute-start.4 = (f32[3,8,1,128]{3,1,2,0:T(8,128)S(1)}, f32[3,8,1,128]{3,1,2,0:T(8,128)S(1)}, u32[]{:S(2)}, u32[]{:S(2)}) collective-permute-start(f32[3,8,1,128]{3,1,2,0:T(8,128)S(1)} %get-tuple-element.68), channel_id=1, source_target_pairs={{0,2},{2,4},{4,6},{6,8},{8,10},{10,12},{12,14},{14,16},{16,18},{18... | collective-permute-start | bytes 36872 | tf_op jit(solution)/shard_map/ppermute | solution.py:23
  29.6 5.6 %collective-permute-start.5 = (f32[3,8,1,128]{3,1,2,0:T(8,128)S(1)}, f32[3,8,1,128]{3,1,2,0:T(8,128)S(1)}, u32[]{:S(2)}, u32[]{:S(2)}) collective-permute-start(f32[3,8,1,128]{3,1,2,0:T(8,128)S(1)} %get-tuple-element.69), channel_id=1, source_target_pairs={{2,0},{4,2},{6,4},{8,6},{10,8},{12,10},{14,12},{16,14},{18,16},{20... | collective-permute-start | bytes 36872 | tf_op jit(solution)/shard_map/ppermute | solution.py:24
  35.3 5.4 %copy-start = (f32[8,16,128]{2,1,0:T(8,128)S(1)}, f32[8,16,128]{2,1,0:T(8,128)}, u32[]{:S(2)}) copy-start(f32[8,16,128]{2,1,0:T(8,128)} %param.11) | copy-start | bytes 196612
  35.3 5.4 %copy-start.3 = (f32[8,16,128]{2,1,0:T(8,128)S(1)}, f32[8,16,128]{2,1,0:T(8,128)}, u32[]{:S(2)}) copy-start(f32[8,16,128]{2,1,0:T(8,128)} %param.10) | copy-start | bytes 196612
  35.3 2.8 %collective-permute-start.6 = (f32[3,8,18,1]{3,1,2,0:T(8,128)S(1)}, f32[3,8,18,1]{3,1,2,0:T(8,128)S(1)}, u32[]{:S(2)}, u32[]{:S(2)}) collective-permute-start(f32[3,8,18,1]{3,1,2,0:T(8,128)S(1)} %get-tuple-element.64), channel_id=1, source_target_pairs={{0,1},{2,3},{4,5},{6,7},{8,9},{10,11},{12,13},{14,15},{16,17},{18,... | collective-permute-start | bytes 5192 | tf_op jit(solution)/shard_map/ppermute | solution.py:23
  36.8 3.4 %collective-permute-start.7 = (f32[3,8,18,1]{3,1,2,0:T(8,128)S(1)}, f32[3,8,18,1]{3,1,2,0:T(8,128)S(1)}, u32[]{:S(2)}, u32[]{:S(2)}) collective-permute-start(f32[3,8,18,1]{3,1,2,0:T(8,128)S(1)} %get-tuple-element.65), channel_id=1, source_target_pairs={{1,0},{3,2},{5,4},{7,6},{9,8},{11,10},{13,12},{15,14},{17,16},{19,... | collective-permute-start | bytes 5192 | tf_op jit(solution)/shard_map/ppermute | solution.py:24
  41.5 7.7 %collective-permute-start.8 = (f32[6,8,1,128]{3,1,2,0:T(8,128)S(1)}, f32[6,8,1,128]{3,1,2,0:T(8,128)S(1)}, u32[]{:S(2)}, u32[]{:S(2)}) collective-permute-start(f32[6,8,1,128]{3,1,2,0:T(8,128)S(1)} %get-tuple-element.54), channel_id=1, source_target_pairs={{0,2},{2,4},{4,6},{6,8},{8,10},{10,12},{12,14},{14,16},{16,18},{18... | collective-permute-start | bytes 73736 | tf_op jit(solution)/shard_map/ppermute | solution.py:23
  45.3 5.7 %collective-permute-start.9 = (f32[6,8,1,128]{3,1,2,0:T(8,128)S(1)}, f32[6,8,1,128]{3,1,2,0:T(8,128)S(1)}, u32[]{:S(2)}, u32[]{:S(2)}) collective-permute-start(f32[6,8,1,128]{3,1,2,0:T(8,128)S(1)} %get-tuple-element.55), channel_id=1, source_target_pairs={{2,0},{4,2},{6,4},{8,6},{10,8},{12,10},{14,12},{16,14},{18,16},{20... | collective-permute-start | bytes 73736 | tf_op jit(solution)/shard_map/ppermute | solution.py:24
  49.2 5.4 %copy-start.4 = (f32[3,16,512]{2,1,0:T(8,128)S(1)}, f32[3,16,512]{2,1,0:T(8,128)}, u32[]{:S(2)}) copy-start(f32[3,16,512]{2,1,0:T(8,128)} %param.14) | copy-start | bytes 294916
  49.2 5.4 %copy-start.6 = (s32[256]{0:T(256)S(1)}, s32[256]{0:T(256)}, u32[]{:S(2)}) copy-start(s32[256]{0:T(256)} %param.12) | copy-start | bytes 3076
  51.7 3.1 %collective-permute-start.10 = (f32[6,8,18,1]{2,1,3,0:T(8,128)S(1)}, f32[6,8,18,1]{2,1,3,0:T(8,128)S(1)}, u32[]{:S(2)}, u32[]{:S(2)}) collective-permute-start(f32[6,8,18,1]{2,1,3,0:T(8,128)S(1)} %copy.103), channel_id=1, source_target_pairs={{0,1},{2,3},{4,5},{6,7},{8,9},{10,11},{12,13},{14,15},{16,17},{18,... | collective-permute-start | bytes 10376 | tf_op jit(solution)/shard_map/ppermute | solution.py:23
  53.3 3.1 %collective-permute-start.11 = (f32[6,8,18,1]{2,1,3,0:T(8,128)S(1)}, f32[6,8,18,1]{2,1,3,0:T(8,128)S(1)}, u32[]{:S(2)}, u32[]{:S(2)}) collective-permute-start(f32[6,8,18,1]{2,1,3,0:T(8,128)S(1)} %copy.104), channel_id=1, source_target_pairs={{1,0},{3,2},{5,4},{7,6},{9,8},{11,10},{13,12},{15,14},{17,16},{19,... | collective-permute-start | bytes 10376 | tf_op jit(solution)/shard_map/ppermute | solution.py:24
  59.8 7.7 %collective-permute-start.12 = (f32[3,8,1,128]{3,1,2,0:T(8,128)S(1)}, f32[3,8,1,128]{3,1,2,0:T(8,128)S(1)}, u32[]{:S(2)}, u32[]{:S(2)}) collective-permute-start(f32[3,8,1,128]{3,1,2,0:T(8,128)S(1)} %get-tuple-element.66), channel_id=1, source_target_pairs={{0,2},{2,4},{4,6},{6,8},{8,10},{10,12},{12,14},{14,16},{16,18},{18... | collective-permute-start | bytes 36872 | tf_op jit(solution)/shard_map/ppermute | solution.py:23
  64.6 5.6 %collective-permute-start.13 = (f32[3,8,1,128]{3,1,2,0:T(8,128)S(1)}, f32[3,8,1,128]{3,1,2,0:T(8,128)S(1)}, u32[]{:S(2)}, u32[]{:S(2)}) collective-permute-start(f32[3,8,1,128]{3,1,2,0:T(8,128)S(1)} %get-tuple-element.67), channel_id=1, source_target_pairs={{2,0},{4,2},{6,4},{8,6},{10,8},{12,10},{14,12},{16,14},{18,16},{20... | collective-permute-start | bytes 36872 | tf_op jit(solution)/shard_map/ppermute | solution.py:24
  70.4 2.6 %collective-permute-start.14 = (f32[3,8,18,1]{3,1,2,0:T(8,128)S(1)}, f32[3,8,18,1]{3,1,2,0:T(8,128)S(1)}, u32[]{:S(2)}, u32[]{:S(2)}) collective-permute-start(f32[3,8,18,1]{3,1,2,0:T(8,128)S(1)} %get-tuple-element.62), channel_id=1, source_target_pairs={{0,1},{2,3},{4,5},{6,7},{8,9},{10,11},{12,13},{14,15},{16,17},{18,... | collective-permute-start | bytes 5192 | tf_op jit(solution)/shard_map/ppermute | solution.py:23
  71.7 3.4 %collective-permute-start.15 = (f32[3,8,18,1]{3,1,2,0:T(8,128)S(1)}, f32[3,8,18,1]{3,1,2,0:T(8,128)S(1)}, u32[]{:S(2)}, u32[]{:S(2)}) collective-permute-start(f32[3,8,18,1]{3,1,2,0:T(8,128)S(1)} %get-tuple-element.63), channel_id=1, source_target_pairs={{1,0},{3,2},{5,4},{7,6},{9,8},{11,10},{13,12},{15,14},{17,16},{19,... | collective-permute-start | bytes 5192 | tf_op jit(solution)/shard_map/ppermute | solution.py:24
  76.4 7.9 %collective-permute-start.16 = (f32[3,2,512]{2,1,0:T(2,128)S(1)}, f32[3,2,512]{2,1,0:T(2,128)S(1)}, u32[]{:S(2)}, u32[]{:S(2)}) collective-permute-start(f32[3,2,512]{2,1,0:T(2,128)S(1)} %get-tuple-element.97), channel_id=1, source_target_pairs={{0,2},{2,4},{4,6},{6,8},{8,10},{10,12},{12,14},{14,16},{16,18},{18... | collective-permute-start | bytes 36872 | tf_op jit(solution)/shard_map/ppermute | solution.py:23
  80.1 5.6 %collective-permute-start.17 = (f32[3,2,512]{2,1,0:T(2,128)S(1)}, f32[3,2,512]{2,1,0:T(2,128)S(1)}, u32[]{:S(2)}, u32[]{:S(2)}) collective-permute-start(f32[3,2,512]{2,1,0:T(2,128)S(1)} %get-tuple-element.98), channel_id=1, source_target_pairs={{2,0},{4,2},{6,4},{8,6},{10,8},{12,10},{14,12},{16,14},{18,16},{20... | collective-permute-start | bytes 36872 | tf_op jit(solution)/shard_map/ppermute | solution.py:24
  84.0 6.5 %copy-start.2 = (f32[16,512]{1,0:T(8,128)S(1)}, f32[16,512]{1,0:T(8,128)}, u32[]{:S(2)}) copy-start(f32[16,512]{1,0:T(8,128)} %param.15) | copy-start | bytes 98308
  85.8 2.8 %collective-permute-start.18 = (f32[3,20,2]{2,1,0:T(8,128)S(1)}, f32[3,20,2]{2,1,0:T(8,128)S(1)}, u32[]{:S(2)}, u32[]{:S(2)}) collective-permute-start(f32[3,20,2]{2,1,0:T(8,128)S(1)} %get-tuple-element.89), channel_id=1, source_target_pairs={{0,1},{2,3},{4,5},{6,7},{8,9},{10,11},{12,13},{14,15},{16,17},{18,... | collective-permute-start | bytes 1448 | tf_op jit(solution)/shard_map/ppermute | solution.py:23
  87.1 3.1 %collective-permute-start.19 = (f32[3,20,2]{2,1,0:T(8,128)S(1)}, f32[3,20,2]{2,1,0:T(8,128)S(1)}, u32[]{:S(2)}, u32[]{:S(2)}) collective-permute-start(f32[3,20,2]{2,1,0:T(8,128)S(1)} %get-tuple-element.90), channel_id=1, source_target_pairs={{1,0},{3,2},{5,4},{7,6},{9,8},{11,10},{13,12},{15,14},{17,16},{19,... | collective-permute-start | bytes 1448 | tf_op jit(solution)/shard_map/ppermute | solution.py:24
  90.7 7.7 %collective-permute-start.20 = (f32[3,2,512]{2,1,0:T(2,128)S(1)}, f32[3,2,512]{2,1,0:T(2,128)S(1)}, u32[]{:S(2)}, u32[]{:S(2)}) collective-permute-start(f32[3,2,512]{2,1,0:T(2,128)S(1)} %get-tuple-element.95), channel_id=1, source_target_pairs={{0,2},{2,4},{4,6},{6,8},{8,10},{10,12},{12,14},{14,16},{16,18},{18... | collective-permute-start | bytes 36872 | tf_op jit(solution)/shard_map/ppermute | solution.py:23
  94.7 5.6 %collective-permute-start.21 = (f32[3,2,512]{2,1,0:T(2,128)S(1)}, f32[3,2,512]{2,1,0:T(2,128)S(1)}, u32[]{:S(2)}, u32[]{:S(2)}) collective-permute-start(f32[3,2,512]{2,1,0:T(2,128)S(1)} %get-tuple-element.96), channel_id=1, source_target_pairs={{2,0},{4,2},{6,4},{8,6},{10,8},{12,10},{14,12},{16,14},{18,16},{20... | collective-permute-start | bytes 36872 | tf_op jit(solution)/shard_map/ppermute | solution.py:24
  100.3 2.6 %collective-permute-start.22 = (f32[3,20,2]{2,1,0:T(8,128)S(1)}, f32[3,20,2]{2,1,0:T(8,128)S(1)}, u32[]{:S(2)}, u32[]{:S(2)}) collective-permute-start(f32[3,20,2]{2,1,0:T(8,128)S(1)} %get-tuple-element.87), channel_id=1, source_target_pairs={{0,1},{2,3},{4,5},{6,7},{8,9},{10,11},{12,13},{14,15},{16,17},{18,... | collective-permute-start | bytes 1448 | tf_op jit(solution)/shard_map/ppermute | solution.py:23
  101.7 3.1 %collective-permute-start.23 = (f32[3,20,2]{2,1,0:T(8,128)S(1)}, f32[3,20,2]{2,1,0:T(8,128)S(1)}, u32[]{:S(2)}, u32[]{:S(2)}) collective-permute-start(f32[3,20,2]{2,1,0:T(8,128)S(1)} %get-tuple-element.88), channel_id=1, source_target_pairs={{1,0},{3,2},{5,4},{7,6},{9,8},{11,10},{13,12},{15,14},{17,16},{19,... | collective-permute-start | bytes 1448 | tf_op jit(solution)/shard_map/ppermute | solution.py:24
  105.2 7.7 %collective-permute-start.24 = (f32[3,2,512]{2,1,0:T(2,128)S(1)}, f32[3,2,512]{2,1,0:T(2,128)S(1)}, u32[]{:S(2)}, u32[]{:S(2)}) collective-permute-start(f32[3,2,512]{2,1,0:T(2,128)S(1)} %get-tuple-element.93), channel_id=1, source_target_pairs={{0,2},{2,4},{4,6},{6,8},{8,10},{10,12},{12,14},{14,16},{16,18},{18... | collective-permute-start | bytes 36872 | tf_op jit(solution)/shard_map/ppermute | solution.py:23
  109.0 5.6 %collective-permute-start.25 = (f32[3,2,512]{2,1,0:T(2,128)S(1)}, f32[3,2,512]{2,1,0:T(2,128)S(1)}, u32[]{:S(2)}, u32[]{:S(2)}) collective-permute-start(f32[3,2,512]{2,1,0:T(2,128)S(1)} %get-tuple-element.94), channel_id=1, source_target_pairs={{2,0},{4,2},{6,4},{8,6},{10,8},{12,10},{14,12},{16,14},{18,16},{20... | collective-permute-start | bytes 36872 | tf_op jit(solution)/shard_map/ppermute | solution.py:24
  114.7 2.6 %collective-permute-start.26 = (f32[3,20,2]{2,1,0:T(8,128)S(1)}, f32[3,20,2]{2,1,0:T(8,128)S(1)}, u32[]{:S(2)}, u32[]{:S(2)}) collective-permute-start(f32[3,20,2]{2,1,0:T(8,128)S(1)} %get-tuple-element.85), channel_id=1, source_target_pairs={{0,1},{2,3},{4,5},{6,7},{8,9},{10,11},{12,13},{14,15},{16,17},{18,... | collective-permute-start | bytes 1448 | tf_op jit(solution)/shard_map/ppermute | solution.py:23
  116.0 3.1 %collective-permute-start.27 = (f32[3,20,2]{2,1,0:T(8,128)S(1)}, f32[3,20,2]{2,1,0:T(8,128)S(1)}, u32[]{:S(2)}, u32[]{:S(2)}) collective-permute-start(f32[3,20,2]{2,1,0:T(8,128)S(1)} %get-tuple-element.86), channel_id=1, source_target_pairs={{1,0},{3,2},{5,4},{7,6},{9,8},{11,10},{13,12},{15,14},{17,16},{19,... | collective-permute-start | bytes 1448 | tf_op jit(solution)/shard_map/ppermute | solution.py:24
  119.6 7.7 %collective-permute-start.28 = (f32[3,2,512]{2,1,0:T(2,128)S(1)}, f32[3,2,512]{2,1,0:T(2,128)S(1)}, u32[]{:S(2)}, u32[]{:S(2)}) collective-permute-start(f32[3,2,512]{2,1,0:T(2,128)S(1)} %get-tuple-element.91), channel_id=1, source_target_pairs={{0,2},{2,4},{4,6},{6,8},{8,10},{10,12},{12,14},{14,16},{16,18},{18... | collective-permute-start | bytes 36872 | tf_op jit(solution)/shard_map/ppermute | solution.py:23
  124.4 5.6 %collective-permute-start.29 = (f32[3,2,512]{2,1,0:T(2,128)S(1)}, f32[3,2,512]{2,1,0:T(2,128)S(1)}, u32[]{:S(2)}, u32[]{:S(2)}) collective-permute-start(f32[3,2,512]{2,1,0:T(2,128)S(1)} %get-tuple-element.92), channel_id=1, source_target_pairs={{2,0},{4,2},{6,4},{8,6},{10,8},{12,10},{14,12},{16,14},{18,16},{20... | collective-permute-start | bytes 36872 | tf_op jit(solution)/shard_map/ppermute | solution.py:24
  130.1 2.6 %collective-permute-start.30 = (f32[3,20,2]{2,1,0:T(8,128)S(1)}, f32[3,20,2]{2,1,0:T(8,128)S(1)}, u32[]{:S(2)}, u32[]{:S(2)}) collective-permute-start(f32[3,20,2]{2,1,0:T(8,128)S(1)} %get-tuple-element.83), channel_id=1, source_target_pairs={{0,1},{2,3},{4,5},{6,7},{8,9},{10,11},{12,13},{14,15},{16,17},{18,... | collective-permute-start | bytes 1448 | tf_op jit(solution)/shard_map/ppermute | solution.py:23
  131.4 3.1 %collective-permute-start.31 = (f32[3,20,2]{2,1,0:T(8,128)S(1)}, f32[3,20,2]{2,1,0:T(8,128)S(1)}, u32[]{:S(2)}, u32[]{:S(2)}) collective-permute-start(f32[3,20,2]{2,1,0:T(8,128)S(1)} %get-tuple-element.84), channel_id=1, source_target_pairs={{1,0},{3,2},{5,4},{7,6},{9,8},{11,10},{13,12},{15,14},{17,16},{19,... | collective-permute-start | bytes 1448 | tf_op jit(solution)/shard_map/ppermute | solution.py:24
  132.7 2.9 %copy-start.5 = (f32[9,8,16,128]{3,2,1,0:T(8,128)}, f32[9,8,16,128]{3,2,1,0:T(8,128)S(1)}, u32[]{:S(2)}) copy-start(f32[9,8,16,128]{3,2,1,0:T(8,128)S(1)} %copy_dynamic-update-slice_fusion.1) | copy-start | bytes 1769476
Sparse Core Ops, SparseCore 0:
  59.7 9.2 reduce-scatter.1
where the time goes:
time: 145 us; the launch traced here: 142 us
  starting transfers between devices  82.2 us (57%)
  waiting for transfers between devices  27.9 us (19%)
  between operations  15 us (10%)
  other arithmetic  8.13 us (6%)
  local copies, waits for them, and re-layouts  7.67 us (5%)
  matrix products  1.46 us (1%)
    ppermute x16, starting transfers between devices, padded(): before = lax.ppermute(last, axis, up)  43 us
    ppermute x16, starting transfers between devices, padded(): after = lax.ppermute(leading, axis, down)  39.2 us
    ppermute x16, waiting for transfers between devices, padded(): after = lax.ppermute(leading, axis, down)  27.8 us
    concatenate x11, other arithmetic, padded(): x = jnp.concatenate([before, x, after], axis=dim)  3.22 us
  transfers between devices with their start and end apart: 33, of which 16 were waited for; matrix products, arithmetic and copies ran while one was open for 3% of the time, Pallas kernels for 0%

commit v1 on v0

v1 whole, which is shorter than its diff:
```python
import functools
import math

import jax
import jax.numpy as jnp
from jax import lax
from jax.experimental import pallas as pl
from jax.experimental.pallas import tpu as pltpu
from jax.sharding import PartitionSpec as P

MESH = pl.DeviceIdType.MESH
WAVE_STEPS = 4
time_step = 0.25
wave_step = 0.5

V1, V2, V3, S11, S22, S33, S23, S13, S12, BUO, LAM, MU = range(12)
FIELDS = 9
ALL = 12
HALO = 2
OHALO = 8
FRONT = 3

SEC_DIRS = (1, -1)


def rows_up(x):
    return pltpu.roll(x, x.shape[0] - 1, 0)


def rows_down(x):
    return pltpu.roll(x, 1, 0)


def lanes_up(x):
    return pltpu.roll(x, x.shape[1] - 1, 1)


def lanes_down(x):
    return pltpu.roll(x, 1, 1)


def kernel_body(
    slab, buoyancy, lame_lambda, lame_mu, face_map, bands, ocean, depth,
    slab_out, ocean_out,
    ext, send_rows, recv_rows, pack, recv_pack, send_corner, recv_corner, ext_pack,
    oext, opack, recv_opack, recv_ocorner, wown, wrecv, uplift, k_hi, k_lo,
    sec_send, sec_recv, blk_send, blk_recv, diag_send, diag_recv, up_send, up_recv,
):
    n_sec = lax.axis_size("sec")
    n_blk = lax.axis_size("blk")
    sec = lax.axis_index("sec")
    blk = lax.axis_index("blk")
    thick, rows, lanes = slab.shape[1:]
    ext_rows = ext.shape[2]
    ocols = ocean.shape[2]
    oext_cols = oext.shape[2]
    tile_cols = bands.shape[1]

    def has_sec(step):
        return sec + step < n_sec if step > 0 else sec + step >= 0

    def has_blk(step):
        return blk + step < n_blk if step > 0 else blk + step >= 0

    recv_rows[...] = jnp.zeros_like(recv_rows)
    recv_pack[...] = jnp.zeros_like(recv_pack)
    recv_corner[...] = jnp.zeros_like(recv_corner)
    recv_opack[...] = jnp.zeros_like(recv_opack)
    recv_ocorner[...] = jnp.zeros_like(recv_ocorner)
    wrecv[...] = jnp.ones_like(wrecv)
    uplift[:, 0:OHALO, :] = jnp.zeros((n_blk, OHALO, lanes), jnp.float32)
    uplift[:, OHALO + rows:, :] = jnp.zeros((n_blk, OHALO, lanes), jnp.float32)
    oext[:, 0:OHALO, 0:ocols] = jnp.zeros((4, OHALO, ocols), jnp.float32)
    oext[:, OHALO + rows:, 0:ocols] = jnp.zeros((4, OHALO, ocols), jnp.float32)

    barrier = pltpu.get_barrier_semaphore()

    def greet(step, turn):
        pl.semaphore_signal(
            barrier, inc=1,
            device_id=(sec + step, lax.rem(blk + turn, n_blk)), device_id_type=MESH,
        )

    for turn in range(1, n_blk):
        greet(0, turn)
    for step in SEC_DIRS:
        @pl.when(has_sec(step))
        def _():
            for turn in range(n_blk):
                greet(step, turn)

    lane = lax.broadcasted_iota(jnp.int32, (rows, lanes), 1)
    sources = [(slab, f) for f in range(FIELDS)] + [
        (buoyancy, None), (lame_lambda, None), (lame_mu, None)]

    def pack_layer(t, carry):
        packed = jnp.zeros((rows, lanes), jnp.float32)
        for f, (ref, at) in enumerate(sources):
            value = ref[t] if at is None else ref[at, t]
            ext[f, t + 1, 0:rows, 0:lanes] = value
            send_rows[0, t, HALO * f:HALO * f + HALO, :] = value[rows - HALO:, :]
            send_rows[1, t, HALO * f:HALO * f + HALO, :] = value[0:HALO, :]
            moved = pltpu.roll(value, 4 * f, 1) if f else value
            packed = jnp.where(((lane - 4 * f + 2) & (lanes - 1)) < 4, moved, packed)
        pack[t] = packed
        send_corner[0, t] = packed[rows - HALO:, :]
        send_corner[1, t] = packed[0:HALO, :]
        return carry

    lax.fori_loop(0, thick, pack_layer, 0)

    opacked = jnp.zeros((rows, lanes), jnp.float32)
    for a in range(4):
        value = ocean[a] if a < 3 else depth[...]
        oext[a, OHALO:OHALO + rows, 0:ocols] = value
        edges = jnp.where(lane < lanes // 2, value[:, 0:lanes], value[:, ocols - lanes:])
        moved = pltpu.roll(edges, 16 * a, 1) if a else edges
        opacked = jnp.where(((lane - 16 * a + 8) & (lanes - 1)) < 16, moved, opacked)
    opack[...] = opacked

    wlane = lax.broadcasted_iota(jnp.int32, wown.shape, 1)
    wvalue = jnp.ones(wown.shape, jnp.float32)
    for j in range(tile_cols):
        wvalue = jnp.where(wlane == j, bands[0:1, j:j + 1].astype(jnp.float32), wvalue)
    wown[...] = wvalue

    near = (n_blk - 1) + sum(
        jnp.where(has_sec(step), n_blk, 0) for step in SEC_DIRS)
    pl.semaphore_wait(barrier, near)

    def sec_copies(d):
        step = SEC_DIRS[d]
        target = (sec + step, blk)
        own_rows = pl.ds(OHALO + rows - OHALO, OHALO) if d == 0 else pl.ds(OHALO, OHALO)
        to_rows = pl.ds(0, OHALO) if d == 0 else pl.ds(OHALO + rows, OHALO)
        pairs = [
            (send_rows.at[d, pl.ds(0, FRONT)], recv_rows.at[d, pl.ds(0, FRONT)]),
            (wown, wrecv.at[d]),
            (send_rows.at[d, pl.ds(FRONT, thick - FRONT)],
             recv_rows.at[d, pl.ds(FRONT, thick - FRONT)]),
            (oext.at[:, own_rows, pl.ds(0, ocols)], oext.at[:, to_rows, pl.ds(0, ocols)]),
        ]
        return [
            pltpu.make_async_remote_copy(
                src_ref=src, dst_ref=dst, send_sem=sec_send.at[d, i], recv_sem=sec_recv.at[d, i],
                device_id=target, device_id_type=MESH)
            for i, (src, dst) in enumerate(pairs)
        ]

    def blk_copies(e):
        target = (sec, blk + SEC_DIRS[e])
        pairs = [(pack, recv_pack.at[e]), (opack, recv_opack.at[e])]
        return [
            pltpu.make_async_remote_copy(
                src_ref=src, dst_ref=dst, send_sem=blk_send.at[e, i], recv_sem=blk_recv.at[e, i],
                device_id=target, device_id_type=MESH)
            for i, (src, dst) in enumerate(pairs)
        ]

    def diag_copies(d, e):
        target = (sec + SEC_DIRS[d], blk + SEC_DIRS[e])
        orows = pl.ds(rows - OHALO, OHALO) if d == 0 else pl.ds(0, OHALO)
        pairs = [
            (send_corner.at[d], recv_corner.at[d, e]),
            (opack.at[orows], recv_ocorner.at[d, e]),
        ]
        return [
            pltpu.make_async_remote_copy(
                src_ref=src, dst_ref=dst, send_sem=diag_send.at[d, e, i],
                recv_sem=diag_recv.at[d, e, i], device_id=target, device_id_type=MESH)
            for i, (src, dst) in enumerate(pairs)
        ]

    def both(d, e):
        return jnp.logical_and(has_sec(SEC_DIRS[d]), has_blk(SEC_DIRS[e]))

    def from_both(d, e):
        return jnp.logical_and(has_sec(-SEC_DIRS[d]), has_blk(-SEC_DIRS[e]))

    def start_at(condition, copies, i):
        @pl.when(condition)
        def _():
            copies[i].start()

    for i in (0,):
        for d in range(2):
            start_at(has_sec(SEC_DIRS[d]), sec_copies(d), 0)
        for d in range(2):
            for e in range(2):
                start_at(both(d, e), diag_copies(d, e), 0)
        for e in range(2):
            start_at(has_blk(SEC_DIRS[e]), blk_copies(e), 0)
    for d in range(2):
        start_at(has_sec(SEC_DIRS[d]), sec_copies(d), 1)
    for d in range(2):
        start_at(has_sec(SEC_DIRS[d]), sec_copies(d), 2)
    for d in range(2):
        start_at(has_sec(SEC_DIRS[d]), sec_copies(d), 3)
        for e in range(2):
            start_at(both(d, e), diag_copies(d, e), 1)
    for e in range(2):
        start_at(has_blk(SEC_DIRS[e]), blk_copies(e), 1)

    for f in range(FIELDS):
        ext[f, 0] = jnp.zeros(ext.shape[2:], jnp.float32)
        ext[f, thick + 1] = jnp.zeros(ext.shape[2:], jnp.float32)

    def make_kernel(band, widths):
        def width_at(step):
            at = lax.broadcasted_iota(jnp.int32, (1, lanes), 1) == blk + step
            total = jnp.sum(jnp.where(at, widths, 0.0), axis=1, keepdims=True)
            return jnp.maximum(total, 1.0)

        def fill(first, column, count, width):
            col = lax.broadcasted_iota(jnp.int32, (count, face_map.shape[1]), 0) + column
            distance = jnp.abs(col - face_map[...]).astype(jnp.float32)
            decay = jnp.exp(distance * (-math.pi / 2.0 / width))
            value = decay / (width + width * (decay * decay))
            high = value.astype(jnp.bfloat16)
            low = (value - high.astype(jnp.float32)).astype(jnp.bfloat16)
            k_hi[band, pl.ds(first, count), :] = high
            k_lo[band, pl.ds(first, count), :] = low

        here = width_at(0)
        chunk = 32

        def some(i, carry):
            fill(pl.multiple_of(i * chunk, chunk), blk * ocols + i * chunk, chunk, here)
            return carry

        lax.fori_loop(0, ocols // chunk, some, 0)
        blank = jnp.zeros((oext_cols - ocols - 32, face_map.shape[1]), jnp.bfloat16)
        k_hi[band, ocols + 16:oext_cols - 16, :] = blank
        k_lo[band, ocols + 16:oext_cols - 16, :] = blank
        fill(ocols, blk * ocols + ocols, 16, width_at(1))
        fill(oext_cols - 16, blk * ocols - 16, 16, width_at(-1))

    make_kernel(1, wown[0:1, :])
    for d in range(2):
        @pl.when(has_sec(-SEC_DIRS[d]))
        def _():
            sec_copies(d)[1].wait_recv()
        make_kernel(2 * d, wrecv[d, 0:1, :])

    def wait_if(condition, copy):
        @pl.when(condition)
        def _():
            copy.wait_recv()

    def assemble(t, carry):
        picks = (lane & 3) < 2
        ext_pack[t, 0:rows, :] = jnp.where(picks, recv_pack[1, t], recv_pack[0, t])
        few = picks[0:HALO]
        after, before = pl.ds(rows, HALO), pl.ds(ext_rows - HALO, HALO)
        ext_pack[t, after, :] = jnp.where(few, recv_corner[1, 1, t], recv_corner[1, 0, t])
        ext_pack[t, before, :] = jnp.where(few, recv_corner[0, 1, t], recv_corner[0, 0, t])
        sides = ext_pack[t]
        for f in range(ALL):
            ext[f, t + 1, after, 0:lanes] = recv_rows[1, t, HALO * f:HALO * f + HALO, :]
            ext[f, t + 1, before, 0:lanes] = recv_rows[0, t, HALO * f:HALO * f + HALO, :]
            ext[f, t + 1, :, lanes:2 * lanes] = (
                pltpu.roll(sides, lanes - 4 * f, 1) if f else sides)
        return carry

    def velocity_1(u, s11, s11_next, s12, s13):
        return ext[V1, u] + time_step * ext[BUO, u] * (
            (s11_next - s11) + (s12 - rows_down(s12)) + (s13 - lanes_down(s13)))

    def velocity(t, carry):
        u = t + 1
        s12, s13, s23 = ext[S12, u], ext[S13, u], ext[S23, u]
        scale = time_step * ext[BUO, u]
        s22, s33 = ext[S22, u], ext[S33, u]
        ext[V1, u] = velocity_1(u, ext[S11, u], ext[S11, u + 1], s12, s13)
        ext[V2, u] = ext[V2, u] + scale * (
            (rows_up(s22) - s22) + (s12 - ext[S12, u - 1]) + (s23 - lanes_down(s23)))
        ext[V3, u] = ext[V3, u] + scale * (
            (lanes_up(s33) - s33) + (s13 - ext[S13, u - 1]) + (s23 - rows_down(s23)))
        return carry

    def strains(u):
        v1, v2, v3 = ext[V1, u], ext[V2, u], ext[V3, u]
        return v1 - ext[V1, u - 1], v2 - rows_down(v2), v3 - lanes_down(v3)

    def stress_values(u):
        v1, v2, v3 = ext[V1, u], ext[V2, u], ext[V3, u]
        e1, e2, e3 = strains(u)
        scale = time_step * ext[MU, u]
        common = time_step * ext[LAM, u] * (e1 + e2 + e3)
        twice = 2.0 * scale
        return (
            (S11, ext[S11, u] + (common + twice * e1)),
            (S22, ext[S22, u] + (common + twice * e2)),
            (S33, ext[S33, u] + (common + twice * e3)),
            (S23, ext[S23, u] + scale * ((lanes_up(v2) - v2) + (rows_up(v3) - v3))),
            (S13, ext[S13, u] + scale * ((lanes_up(v1) - v1) + (ext[V3, u + 1] - v3))),
            (S12, ext[S12, u] + scale * ((rows_up(v1) - v1) + (ext[V2, u + 1] - v2))),
        )

    def stress(t, carry):
        for f, value in stress_values(t + 1):
            ext[f, t + 1] = value
        return carry

    def last_stress(t, carry):
        for f in (V1, V2, V3):
            slab_out[f, t] = ext[f, t + 1, 0:rows, 0:lanes]
        for f, value in stress_values(t + 1):
            slab_out[f, t] = value[0:rows, 0:lanes]
        return carry

    for d in range(2):
        wait_if(has_sec(-SEC_DIRS[d]), sec_copies(d)[0])
        for e in range(2):
            wait_if(from_both(d, e), diag_copies(d, e)[0])
    for e in range(2):
        wait_if(has_blk(-SEC_DIRS[e]), blk_copies(e)[0])
    lax.fori_loop(0, FRONT, assemble, 0)
    velocity(0, 0)
    velocity(1, 0)
    stress(0, 0)
    e1, e2, e3 = strains(2)
    s11_next = ext[S11, 2] + time_step * (
        ext[LAM, 2] * (e1 + e2 + e3) + 2.0 * ext[MU, 2] * e1)
    second = velocity_1(1, ext[S11, 1], s11_next, ext[S12, 1], ext[S13, 1])
    rise = time_step * (ext[V1, 1] + second)
    uplift[blk, OHALO:OHALO + rows, :] = rise[0:rows, 0:lanes]

    own_rows = pl.ds(OHALO, rows)

    def up_copy(d, turn):
        step = (1, -1, 0)[d]
        src = (pl.ds(OHALO + rows - OHALO, OHALO), pl.ds(OHALO, OHALO), own_rows)[d]
        dst = (pl.ds(0, OHALO), pl.ds(OHALO + rows, OHALO), own_rows)[d]
        return pltpu.make_async_remote_copy(
            src_ref=uplift.at[blk, src], dst_ref=uplift.at[blk, dst],
            send_sem=up_send.at[d, turn], recv_sem=up_recv.at[d, turn],
            device_id=(sec + step, lax.rem(blk + turn, n_blk)), device_id_type=MESH)

    def up_arrival(d, turn):
        owner = lax.rem(blk + n_blk - turn, n_blk)
        step = (1, -1, 0)[d]
        dst = (pl.ds(0, OHALO), pl.ds(OHALO + rows, OHALO), own_rows)[d]
        return pltpu.make_async_remote_copy(
            src_ref=uplift.at[owner, dst], dst_ref=uplift.at[owner, dst],
            send_sem=up_send.at[d, turn], recv_sem=up_recv.at[d, turn],
            device_id=(sec + step, lax.rem(blk + turn, n_blk)), device_id_type=MESH)

    for d in range(2):
        @pl.when(has_sec(SEC_DIRS[d]))
        def _():
            for turn in range(n_blk):
                up_copy(d, turn).start()
    for turn in range(1, n_blk):
        up_copy(2, turn).start()

    for d in range(2):
        wait_if(has_sec(-SEC_DIRS[d]), sec_copies(d)[2])
    lax.fori_loop(FRONT, thick, assemble, 0)
    lax.fori_loop(2, thick, velocity, 0)
    lax.fori_loop(1, thick, stress, 0)
    lax.fori_loop(0, thick, velocity, 0)
    lax.fori_loop(0, thick, last_stress, 0)

    for d in range(2):
        @pl.when(has_sec(-SEC_DIRS[d]))
        def _():
            sec_copies(d)[3].wait_recv()
            for turn in range(n_blk):
                up_arrival(d, turn).wait_recv()
        for e in range(2):
            wait_if(from_both(d, e), diag_copies(d, e)[1])
    for turn in range(1, n_blk):
        up_arrival(2, turn).wait_recv()
    for e in range(2):
        wait_if(has_blk(-SEC_DIRS[e]), blk_copies(e)[1])

    all_rows = rows + 2 * OHALO
    right = (lax.broadcasted_iota(jnp.int32, (rows, lanes), 1) & 15) < 8
    side_rows = jnp.concatenate([
        jnp.where(right[0:OHALO], recv_ocorner[0, 1], recv_ocorner[0, 0]),
        jnp.where(right, recv_opack[1], recv_opack[0]),
        jnp.where(right[0:OHALO], recv_ocorner[1, 1], recv_ocorner[1, 0]),
    ], axis=0)
    state = []
    for a in range(4):
        sides = pltpu.roll(side_rows, lanes - 16 * a, 1) if a else side_rows
        state.append(jnp.concatenate([oext[a, :, 0:ocols], sides], axis=1))
    surface, flux_strike, flux_dip, still = state

    whole = jnp.concatenate([uplift[b] for b in range(n_blk)], axis=1)
    high = whole.astype(jnp.bfloat16)
    low = (whole - high.astype(jnp.float32)).astype(jnp.bfloat16)
    stacked = jnp.concatenate([high, low], axis=0)

    def filtered(band):
        dims = (((1,), (1,)), ((), ()))
        first = lax.dot_general(stacked, k_hi[band], dims, preferred_element_type=jnp.float32)
        second = lax.dot_general(high, k_lo[band], dims, preferred_element_type=jnp.float32)
        return first[0:all_rows] + (first[all_rows:] + second)

    source = jnp.concatenate([
        filtered(0)[0:OHALO], filtered(1)[OHALO:OHALO + rows], filtered(2)[OHALO + rows:]], axis=0)

    row_at = lax.broadcasted_iota(jnp.int32, (all_rows, oext_cols), 0) + (sec * rows - OHALO)
    col = lax.broadcasted_iota(jnp.int32, (all_rows, oext_cols), 1)
    col_at = jnp.where(col < ocols + lanes // 2, col, col - oext_cols) + blk * ocols
    wet = ((row_at >= 0) & (row_at < n_sec * rows)) & ((col_at >= 0) & (col_at < n_blk * ocols))
    surface = jnp.where(wet, surface + source, 0.0)
    pull = wave_step * 0.5 * still
    for _ in range(WAVE_STEPS):
        change = (rows_up(flux_strike) - rows_down(flux_strike)) + (
            lanes_up(flux_dip) - lanes_down(flux_dip))
        surface = jnp.where(wet, surface - wave_step * 0.5 * change, 0.0)
        flux_strike = flux_strike - pull * (rows_up(surface) - rows_down(surface))
        flux_dip = flux_dip - pull * (lanes_up(surface) - lanes_down(surface))
    for a, value in enumerate((surface, flux_strike, flux_dip)):
        ocean_out[a] = value[OHALO:OHALO + rows, 0:ocols]

    for d in range(2):
        @pl.when(has_sec(SEC_DIRS[d]))
        def _():
            for copy in sec_copies(d):
                copy.wait_send()
            for turn in range(n_blk):
                up_copy(d, turn).wait_send()
        for e in range(2):
            @pl.when(both(d, e))
            def _():
                for copy in diag_copies(d, e):
                    copy.wait_send()
    for e in range(2):
        @pl.when(has_blk(SEC_DIRS[e]))
        def _():
            for copy in blk_copies(e):
                copy.wait_send()
    for turn in range(1, n_blk):
        up_copy(2, turn).wait_send()


def on_device(
    slab_state, buoyancy, lame_lambda, lame_mu, face_map, band_widths, ocean_state, water_depth
):
    n_blk = lax.axis_size("blk")
    thick, rows, lanes = slab_state.shape[1:]
    ocols = ocean_state.shape[2]
    dip = face_map.shape[0]
    ext_rows = rows + 8
    oext_cols = ocols + lanes
    f32 = jnp.float32
    vmem = pl.BlockSpec(memory_space=pltpu.VMEM)
    dma = pltpu.SemaphoreType.DMA
    return pl.pallas_call(
        kernel_body,
        out_shape=(
            jax.ShapeDtypeStruct(slab_state.shape, f32),
            jax.ShapeDtypeStruct(ocean_state.shape, f32),
        ),
        in_specs=[vmem] * 8,
        out_specs=(vmem, vmem),
        scratch_shapes=[
            pltpu.VMEM((ALL, thick + 2, ext_rows, 2 * lanes), f32),
            pltpu.VMEM((2, thick, ALL * HALO, lanes), f32),
            pltpu.VMEM((2, thick, ALL * HALO, lanes), f32),
            pltpu.VMEM((thick, rows, lanes), f32),
            pltpu.VMEM((2, thick, rows, lanes), f32),
            pltpu.VMEM((2, thick, HALO, lanes), f32),
            pltpu.VMEM((2, 2, thick, HALO, lanes), f32),
            pltpu.VMEM((thick, ext_rows, lanes), f32),
            pltpu.VMEM((4, rows + 2 * OHALO, oext_cols), f32),
            pltpu.VMEM((rows, lanes), f32),
            pltpu.VMEM((2, rows, lanes), f32),
            pltpu.VMEM((2, 2, OHALO, lanes), f32),
            pltpu.VMEM((8, lanes), f32),
            pltpu.VMEM((2, 8, lanes), f32),
            pltpu.VMEM((n_blk, rows + 2 * OHALO, lanes), f32),
            pltpu.VMEM((3, oext_cols, dip), jnp.bfloat16),
            pltpu.VMEM((3, oext_cols, dip), jnp.bfloat16),
            dma((2, 4)), dma((2, 4)),
            dma((2, 2)), dma((2, 2)),
            dma((2, 2, 2)), dma((2, 2, 2)),
            dma((3, n_blk)), dma((3, n_blk)),
        ],
        compiler_params=pltpu.CompilerParams(
            collective_id=0, has_side_effects=True, vmem_limit_bytes=40 * 1024 * 1024
        ),
        cost_estimate=pl.CostEstimate(
            flops=200_000_000, bytes_accessed=2_000_000, transcendentals=500_000),
    )(
        slab_state, buoyancy, lame_lambda, lame_mu, face_map.reshape(1, dip), band_widths,
        ocean_state, water_depth,
    )


def solution(mesh):
    in_specs = (
        P(None, None, "sec", "blk"),
        P(None, "sec", "blk"),
        P(None, "sec", "blk"),
        P(None, "sec", "blk"),
        P(),
        P("sec", None),
        P(None, "sec", "blk"),
        P("sec", "blk"),
    )
    out_specs = (P(None, None, "sec", "blk"), P(None, "sec", "blk"))
    return jax.shard_map(
        on_device, mesh=mesh, in_specs=in_specs, out_specs=out_specs, check_vma=False
    )
```

time: 145 us -> 25 us (0.17)
  the two profiles are of different devices: /device:TPU:8 before, /device:TPU:17 now
where the time goes in v1:
time: 25 us; the launch traced here: 24.6 us
  Pallas kernels  16.6 us (66%)
  local copies, waits for them, and re-layouts  7.37 us (29%)
  between operations  0.66 us (3%)
    pallas_call x1, Pallas kernels, on_device(): pl.pallas_call(kernel_body, out_shape=(jax.ShapeDtypeStruct(slab_state.sh...  16.6 us
    unnamed x18, local copies, waits for them, and re-layouts  7.37 us

profile of v1, /device:TPU:17, one launch (start us, length us, event | category | flops | bytes accessed | tf_op | source)
XLA Modules:
  0.0 24.6 jit_solution(4392741130562571671)
XLA Ops:
  0.6 0.0 copy-start.7
  0.6 0.0 copy-start.6
  0.7 0.6 %copy-done.7 = s32[1,2]{1,0:T(1,128)S(1)} copy-done((s32[1,2]{1,0:T(1,128)S(1)}, s32[1,2]{1,0:T(1,128)}, u32[]{:S(2)}) %copy-start.7) | copy-done | bytes 32
  1.3 0.0 copy-done.6
  1.3 0.0 copy-start
  1.3 1.1 %copy-done = f32[9,8,16,128]{3,2,1,0:T(8,128)S(1)} copy-done((f32[9,8,16,128]{3,2,1,0:T(8,128)S(1)}, f32[9,8,16,128]{3,2,1,0:T(8,128)}, u32[]{:S(2)}) %copy-start) | copy-done | bytes 589848
  2.4 0.0 copy-start.1
  2.4 0.9 %copy-done.1 = f32[3,16,512]{2,1,0:T(8,128)S(1)} copy-done((f32[3,16,512]{2,1,0:T(8,128)S(1)}, f32[3,16,512]{2,1,0:T(8,128)}, u32[]{:S(2)}) %copy-start.1) | copy-done | bytes 98328
  3.3 0.0 copy-start.2
  3.3 0.8 %copy-done.2 = f32[8,16,128]{2,1,0:T(8,128)S(1)} copy-done((f32[8,16,128]{2,1,0:T(8,128)S(1)}, f32[8,16,128]{2,1,0:T(8,128)}, u32[]{:S(2)}) %copy-start.2) | copy-done | bytes 65560
  4.1 0.0 copy-start.3
  4.1 0.8 %copy-done.3 = f32[8,16,128]{2,1,0:T(8,128)S(1)} copy-done((f32[8,16,128]{2,1,0:T(8,128)S(1)}, f32[8,16,128]{2,1,0:T(8,128)}, u32[]{:S(2)}) %copy-start.3) | copy-done | bytes 65560
  5.0 0.0 copy-start.4
  5.0 0.8 %copy-done.4 = f32[8,16,128]{2,1,0:T(8,128)S(1)} copy-done((f32[8,16,128]{2,1,0:T(8,128)S(1)}, f32[8,16,128]{2,1,0:T(8,128)}, u32[]{:S(2)}) %copy-start.4) | copy-done | bytes 65560
  5.8 0.0 copy-start.5
  5.8 0.8 %copy-done.5 = f32[16,512]{1,0:T(8,128)S(1)} copy-done((f32[16,512]{1,0:T(8,128)S(1)}, f32[16,512]{1,0:T(8,128)}, u32[]{:S(2)}) %copy-start.5) | copy-done | bytes 32792
  6.6 16.6 %shard_map.95 = (f32[9,8,16,128]{3,2,1,0:T(8,128)S(1)}, f32[3,16,512]{2,1,0:T(8,128)S(1)}) custom-call(f32[9,8,16,128]{3,2,1,0:T(8,128)S(1)} %copy-done, f32[8,16,128]{2,1,0:T(8,128)S(1)} %copy-done.2, f32[8,16,128]{2,1,0:T(8,128)S(1)} %copy-done.3, f32[8,16,128]{2,1,0:T(8,128)S(1)} %copy-done.4, s32[1,256]{1,0:T(1,128)S(1)} %bitcast.1, ...), custom_call_target="tpu_custom_call" | custom-call | flops 200000000 | bytes 2000000 | tf_op jit(solution)/shard_map/pallas_call | solution.py:453
  23.1 0.8 %copy.12 = f32[9,8,16,128]{3,2,1,0:T(8,128)} copy(f32[9,8,16,128]{3,2,1,0:T(8,128)S(1)} %get-tuple-element.4) | data formatting | bytes 1179648
  24.0 0.6 %copy.13 = f32[3,16,512]{2,1,0:T(8,128)} copy(f32[3,16,512]{2,1,0:T(8,128)S(1)} %get-tuple-element.5) | data formatting | bytes 196608
Async XLA Ops:
  0.6 0.7 %copy-start.7 = (s32[1,2]{1,0:T(1,128)S(1)}, s32[1,2]{1,0:T(1,128)}, u32[]{:S(2)}) copy-start(s32[1,2]{1,0:T(1,128)} %bands.1) | copy-start | bytes 28
  0.6 0.7 %copy-start.6 = (s32[256]{0:T(256)S(1)}, s32[256]{0:T(256)}, u32[]{:S(2)}) copy-start(s32[256]{0:T(256)} %param.12) | copy-start | bytes 3076
  1.3 1.1 %copy-start = (f32[9,8,16,128]{3,2,1,0:T(8,128)S(1)}, f32[9,8,16,128]{3,2,1,0:T(8,128)}, u32[]{:S(2)}) copy-start(f32[9,8,16,128]{3,2,1,0:T(8,128)} %slab.1) | copy-start | bytes 1769476
  2.4 0.9 %copy-start.1 = (f32[3,16,512]{2,1,0:T(8,128)S(1)}, f32[3,16,512]{2,1,0:T(8,128)}, u32[]{:S(2)}) copy-start(f32[3,16,512]{2,1,0:T(8,128)} %ocean.1) | copy-start | bytes 294916
  3.3 0.8 %copy-start.2 = (f32[8,16,128]{2,1,0:T(8,128)S(1)}, f32[8,16,128]{2,1,0:T(8,128)}, u32[]{:S(2)}) copy-start(f32[8,16,128]{2,1,0:T(8,128)} %buoyancy.1) | copy-start | bytes 196612
  4.1 0.8 %copy-start.3 = (f32[8,16,128]{2,1,0:T(8,128)S(1)}, f32[8,16,128]{2,1,0:T(8,128)}, u32[]{:S(2)}) copy-start(f32[8,16,128]{2,1,0:T(8,128)} %lame_lambda.1) | copy-start | bytes 196612
  5.0 0.8 %copy-start.4 = (f32[8,16,128]{2,1,0:T(8,128)S(1)}, f32[8,16,128]{2,1,0:T(8,128)}, u32[]{:S(2)}) copy-start(f32[8,16,128]{2,1,0:T(8,128)} %lame_mu.1) | copy-start | bytes 196612
  5.8 0.8 %copy-start.5 = (f32[16,512]{1,0:T(8,128)S(1)}, f32[16,512]{1,0:T(8,128)}, u32[]{:S(2)}) copy-start(f32[16,512]{1,0:T(8,128)} %depth.1) | copy-start | bytes 98308

commit v2 on v1

v2 whole, which is shorter than its diff:
```python
import functools
import math

import jax
import jax.numpy as jnp
from jax import lax
from jax.experimental import pallas as pl
from jax.experimental.pallas import tpu as pltpu
from jax.sharding import PartitionSpec as P

MESH = pl.DeviceIdType.MESH
WAVE_STEPS = 4
time_step = 0.25
wave_step = 0.5

V1, V2, V3, S11, S22, S33, S23, S13, S12, BUO, LAM, MU = range(12)
FIELDS = 9
ALL = 12
HALO = 2
OHALO = 8
FRONT = 3

SEC_DIRS = (1, -1)


def rows_up(x):
    return pltpu.roll(x, x.shape[0] - 1, 0)


def rows_down(x):
    return pltpu.roll(x, 1, 0)


def lanes_up(x):
    return pltpu.roll(x, x.shape[1] - 1, 1)


def lanes_down(x):
    return pltpu.roll(x, 1, 1)


def kernel_body(
    slab, buoyancy, lame_lambda, lame_mu, face_hbm, bands_hbm, ocean, depth,
    slab_out, ocean_out,
    ext, send_rows, recv_rows, pack, recv_pack, send_corner, recv_corner, ext_pack,
    oext, opack, recv_opack, recv_ocorner, face_map, bands, uplift, source, k_hi, k_lo,
    load_sem, sec_send, sec_recv, blk_send, blk_recv, diag_send, diag_recv,
    up_send, up_recv, src_send, src_recv,
):
    n_sec = lax.axis_size("sec")
    n_blk = lax.axis_size("blk")
    sec = lax.axis_index("sec")
    blk = lax.axis_index("blk")
    thick, rows, lanes = slab.shape[1:]
    ext_rows = ext.shape[2]
    ocols = ocean.shape[2]
    oext_cols = oext.shape[2]
    dip = face_map.shape[1]
    tile_cols = bands.shape[1]
    front, back = pl.ds(0, FRONT), pl.ds(FRONT, thick - FRONT)

    def has_sec(step):
        return sec + step < n_sec if step > 0 else sec + step >= 0

    def has_blk(step):
        return blk + step < n_blk if step > 0 else blk + step >= 0

    own_rows, own_lanes = pl.ds(0, rows), pl.ds(0, lanes)
    ocean_rows, ocean_cols = pl.ds(OHALO, rows), pl.ds(0, ocols)
    layers = pl.ds(1, thick)
    loads = [
        (slab, ext.at[pl.ds(0, FIELDS), layers, own_rows, own_lanes]),
        (buoyancy, ext.at[BUO, layers, own_rows, own_lanes]),
        (lame_lambda, ext.at[LAM, layers, own_rows, own_lanes]),
        (lame_mu, ext.at[MU, layers, own_rows, own_lanes]),
        (face_hbm, face_map),
        (bands_hbm, bands),
        (ocean, oext.at[pl.ds(0, 3), ocean_rows, ocean_cols]),
        (depth, oext.at[3, ocean_rows, ocean_cols]),
    ]
    loads = [pltpu.make_async_copy(src, dst, load_sem.at[i]) for i, (src, dst) in enumerate(loads)]
    for load in loads:
        load.start()

    recv_rows[...] = jnp.zeros_like(recv_rows)
    recv_pack[...] = jnp.zeros_like(recv_pack)
    recv_corner[...] = jnp.zeros_like(recv_corner)
    recv_opack[...] = jnp.zeros_like(recv_opack)
    recv_ocorner[...] = jnp.zeros_like(recv_ocorner)
    for first in (0, OHALO + rows):
        source[first:first + OHALO, :] = jnp.zeros((OHALO, oext_cols), jnp.float32)
        oext[:, first:first + OHALO, 0:ocols] = jnp.zeros((4, OHALO, ocols), jnp.float32)

    barrier = pltpu.get_barrier_semaphore()

    def greet(step, turn):
        pl.semaphore_signal(
            barrier, inc=1,
            device_id=(sec + step, lax.rem(blk + turn, n_blk)), device_id_type=MESH,
        )

    for turn in range(1, n_blk):
        greet(0, turn)
    for step in SEC_DIRS:
        @pl.when(has_sec(step))
        def _():
            for turn in range(n_blk):
                greet(step, turn)

    for f in range(FIELDS):
        ext[f, 0] = jnp.zeros(ext.shape[2:], jnp.float32)
        ext[f, thick + 1] = jnp.zeros(ext.shape[2:], jnp.float32)

    def remote(src, dst, send_sem, recv_sem, target):
        return pltpu.make_async_remote_copy(
            src_ref=src, dst_ref=dst, send_sem=send_sem, recv_sem=recv_sem,
            device_id=target, device_id_type=MESH)

    def sec_copy(d, i):
        out_rows = pl.ds(rows, OHALO) if d == 0 else pl.ds(OHALO, OHALO)
        to_rows = pl.ds(0, OHALO) if d == 0 else pl.ds(OHALO + rows, OHALO)
        if i == 2:
            src, dst = oext.at[:, out_rows, ocean_cols], oext.at[:, to_rows, ocean_cols]
        else:
            part = (front, back)[i]
            src, dst = send_rows.at[d, part], recv_rows.at[d, part]
        return remote(src, dst, sec_send.at[d, i], sec_recv.at[d, i], (sec + SEC_DIRS[d], blk))

    def blk_copy(e, i):
        if i == 2:
            src, dst = opack, recv_opack.at[e]
        else:
            part = (front, back)[i]
            src, dst = pack.at[part], recv_pack.at[e, part]
        return remote(src, dst, blk_send.at[e, i], blk_recv.at[e, i], (sec, blk + SEC_DIRS[e]))

    def diag_copy(d, e, i):
        if i == 2:
            src = opack.at[pl.ds(rows - OHALO, OHALO) if d == 0 else pl.ds(0, OHALO)]
            dst = recv_ocorner.at[d, e]
        else:
            part = (front, back)[i]
            src, dst = send_corner.at[d, part], recv_corner.at[d, e, part]
        return remote(src, dst, diag_send.at[d, e, i], diag_recv.at[d, e, i],
                      (sec + SEC_DIRS[d], blk + SEC_DIRS[e]))

    def both(d, e):
        return jnp.logical_and(has_sec(SEC_DIRS[d]), has_blk(SEC_DIRS[e]))

    def from_both(d, e):
        return jnp.logical_and(has_sec(-SEC_DIRS[d]), has_blk(-SEC_DIRS[e]))

    def send_all(i):
        for d in range(2):
            @pl.when(has_sec(SEC_DIRS[d]))
            def _():
                sec_copy(d, i).start()
        for d in range(2):
            for e in range(2):
                @pl.when(both(d, e))
                def _():
                    diag_copy(d, e, i).start()
        for e in range(2):
            @pl.when(has_blk(SEC_DIRS[e]))
            def _():
                blk_copy(e, i).start()

    def await_all(i):
        for d in range(2):
            @pl.when(has_sec(-SEC_DIRS[d]))
            def _():
                sec_copy(d, i).wait_recv()
            for e in range(2):
                @pl.when(from_both(d, e))
                def _():
                    diag_copy(d, e, i).wait_recv()
        for e in range(2):
            @pl.when(has_blk(-SEC_DIRS[e]))
            def _():
                blk_copy(e, i).wait_recv()

    lane = lax.broadcasted_iota(jnp.int32, (rows, lanes), 1)

    def pack_layer(t):
        packed = jnp.zeros((rows, lanes), jnp.float32)
        for f in range(ALL):
            value = ext[f, t + 1, 0:rows, 0:lanes]
            send_rows[0, t, HALO * f:HALO * f + HALO, :] = value[rows - HALO:, :]
            send_rows[1, t, HALO * f:HALO * f + HALO, :] = value[0:HALO, :]
            moved = pltpu.roll(value, 4 * f, 1) if f else value
            packed = jnp.where(((lane - 4 * f + 2) & (lanes - 1)) < 4, moved, packed)
        pack[t] = packed
        send_corner[0, t] = packed[rows - HALO:, :]
        send_corner[1, t] = packed[0:HALO, :]

    for load in loads[:4]:
        load.wait()
    for t in range(FRONT):
        pack_layer(t)
    near = (n_blk - 1) + sum(jnp.where(has_sec(step), n_blk, 0) for step in SEC_DIRS)
    pl.semaphore_wait(barrier, near)
    send_all(0)
    for t in range(FRONT, thick):
        pack_layer(t)
    send_all(1)

    for load in loads[4:]:
        load.wait()
    opacked = jnp.zeros((rows, lanes), jnp.float32)
    for a in range(4):
        value = oext[a, OHALO:OHALO + rows, 0:ocols]
        edges = jnp.where(lane < lanes // 2, value[:, 0:lanes], value[:, ocols - lanes:])
        moved = pltpu.roll(edges, 16 * a, 1) if a else edges
        opacked = jnp.where(((lane - 16 * a + 8) & (lanes - 1)) < 16, moved, opacked)
    opack[...] = opacked
    send_all(2)

    def width_at(step):
        total = jnp.zeros((1, 1), jnp.float32)
        for j in range(tile_cols):
            total = jnp.where(blk + step == j, bands[0:1, j:j + 1].astype(jnp.float32), total)
        return jnp.maximum(total, 1.0)

    chunk = 32
    face = face_map[...].astype(jnp.float32)
    index = lax.broadcasted_iota(jnp.int32, (chunk, dip), 0).astype(jnp.float32)
    own_column = (blk * ocols).astype(jnp.float32)

    def fill(first, column, count, width):
        distance = jnp.abs((index[0:count] + (own_column + float(column))) - face)
        decay = jnp.exp2(distance * (-math.pi / 2.0 * math.log2(math.e) / width))
        under = width + width * (decay * decay)
        guess = pl.reciprocal(under, approx=True)
        value = decay * (guess * (2.0 - under * guess))
        high = value.astype(jnp.bfloat16)
        k_hi[first:first + count, :] = high
        k_lo[first:first + count, :] = (value - high.astype(jnp.float32)).astype(jnp.bfloat16)

    here = width_at(0)
    for first in range(0, ocols, chunk):
        fill(first, first, chunk, here)
    fill(ocols, ocols, 16, width_at(1))
    fill(oext_cols - 16, -16, 16, width_at(-1))
    blank = jnp.zeros((oext_cols - ocols - 32, dip), jnp.bfloat16)
    k_hi[ocols + 16:oext_cols - 16, :] = blank
    k_lo[ocols + 16:oext_cols - 16, :] = blank

    picks = (lane & 3) < 2

    def assemble(t):
        ext_pack[t, 0:rows, :] = jnp.where(picks, recv_pack[1, t], recv_pack[0, t])
        few = picks[0:HALO]
        after, before = pl.ds(rows, HALO), pl.ds(ext_rows - HALO, HALO)
        ext_pack[t, after, :] = jnp.where(few, recv_corner[1, 1, t], recv_corner[1, 0, t])
        ext_pack[t, before, :] = jnp.where(few, recv_corner[0, 1, t], recv_corner[0, 0, t])
        sides = ext_pack[t]
        for f in range(ALL):
            ext[f, t + 1, after, 0:lanes] = recv_rows[1, t, HALO * f:HALO * f + HALO, :]
            ext[f, t + 1, before, 0:lanes] = recv_rows[0, t, HALO * f:HALO * f + HALO, :]
            ext[f, t + 1, :, lanes:2 * lanes] = (
                pltpu.roll(sides, lanes - 4 * f, 1) if f else sides)

    def velocity_1(u, s11, s11_next, s12, s13):
        return ext[V1, u] + time_step * ext[BUO, u] * (
            (s11_next - s11) + (s12 - rows_down(s12)) + (s13 - lanes_down(s13)))

    def velocity(t):
        u = t + 1
        s12, s13, s23 = ext[S12, u], ext[S13, u], ext[S23, u]
        scale = time_step * ext[BUO, u]
        s22, s33 = ext[S22, u], ext[S33, u]
        ext[V1, u] = velocity_1(u, ext[S11, u], ext[S11, u + 1], s12, s13)
        ext[V2, u] = ext[V2, u] + scale * (
            (rows_up(s22) - s22) + (s12 - ext[S12, u - 1]) + (s23 - lanes_down(s23)))
        ext[V3, u] = ext[V3, u] + scale * (
            (lanes_up(s33) - s33) + (s13 - ext[S13, u - 1]) + (s23 - rows_down(s23)))

    def strains(u):
        v1, v2, v3 = ext[V1, u], ext[V2, u], ext[V3, u]
        return v1 - ext[V1, u - 1], v2 - rows_down(v2), v3 - lanes_down(v3)

    def stress_values(u):
        v1, v2, v3 = ext[V1, u], ext[V2, u], ext[V3, u]
        e1, e2, e3 = strains(u)
        scale = time_step * ext[MU, u]
        common = time_step * ext[LAM, u] * (e1 + e2 + e3)
        twice = 2.0 * scale
        return (
            (S11, ext[S11, u] + (common + twice * e1)),
            (S22, ext[S22, u] + (common + twice * e2)),
            (S33, ext[S33, u] + (common + twice * e3)),
            (S23, ext[S23, u] + scale * ((lanes_up(v2) - v2) + (rows_up(v3) - v3))),
            (S13, ext[S13, u] + scale * ((lanes_up(v1) - v1) + (ext[V3, u + 1] - v3))),
            (S12, ext[S12, u] + scale * ((rows_up(v1) - v1) + (ext[V2, u + 1] - v2))),
        )

    def stress(t):
        for f, value in stress_values(t + 1):
            ext[f, t + 1] = value

    def last_stress(t):
        for f in (V1, V2, V3):
            slab_out[f, t] = ext[f, t + 1, 0:rows, 0:lanes]
        for f, value in stress_values(t + 1):
            slab_out[f, t] = value[0:rows, 0:lanes]

    await_all(0)
    for t in range(FRONT):
        assemble(t)
    velocity(0)
    velocity(1)
    stress(0)
    e1, e2, e3 = strains(2)
    s11_next = ext[S11, 2] + time_step * (
        ext[LAM, 2] * (e1 + e2 + e3) + 2.0 * ext[MU, 2] * e1)
    second = velocity_1(1, ext[S11, 1], s11_next, ext[S12, 1], ext[S13, 1])
    rise = time_step * (ext[V1, 1] + second)
    uplift[blk] = rise[0:rows, 0:lanes]

    def up_copy(turn):
        return remote(uplift.at[blk], uplift.at[blk], up_send.at[turn], up_recv.at[turn],
                      (sec, lax.rem(blk + turn, n_blk)))

    def up_arrival(turn):
        owner = lax.rem(blk + n_blk - turn, n_blk)
        return remote(uplift.at[owner], uplift.at[owner], up_send.at[turn], up_recv.at[turn],
                      (sec, lax.rem(blk + turn, n_blk)))

    for turn in range(1, n_blk):
        up_copy(turn).start()

    await_all(1)
    for t in range(FRONT, thick):
        assemble(t)
    for t in range(2, thick):
        velocity(t)
    for t in range(1, thick):
        stress(t)

    for turn in range(1, n_blk):
        up_arrival(turn).wait_recv()
    whole = jnp.concatenate([uplift[b] for b in range(n_blk)], axis=1)
    high = whole.astype(jnp.bfloat16)
    low = (whole - high.astype(jnp.float32)).astype(jnp.bfloat16)
    dims = (((1,), (1,)), ((), ()))
    by_high = lax.dot_general(jnp.concatenate([high, low], axis=0), k_hi[...], dims,
                              preferred_element_type=jnp.float32)
    by_low = lax.dot_general(high, k_lo[...], dims, preferred_element_type=jnp.float32)
    source[OHALO:OHALO + rows, :] = by_high[0:rows] + (by_high[rows:] + by_low)

    def src_copy(d):
        out_rows = pl.ds(rows, OHALO) if d == 0 else pl.ds(OHALO, OHALO)
        to_rows = pl.ds(0, OHALO) if d == 0 else pl.ds(OHALO + rows, OHALO)
        return remote(source.at[out_rows], source.at[to_rows], src_send.at[d], src_recv.at[d],
                      (sec + SEC_DIRS[d], blk))

    for d in range(2):
        @pl.when(has_sec(SEC_DIRS[d]))
        def _():
            src_copy(d).start()

    for t in range(thick):
        velocity(t)
    for t in range(thick):
        last_stress(t)

    await_all(2)
    for d in range(2):
        @pl.when(has_sec(-SEC_DIRS[d]))
        def _():
            src_copy(d).wait_recv()

    all_rows = rows + 2 * OHALO
    right = (lane & 15) < 8
    side_rows = jnp.concatenate([
        jnp.where(right[0:OHALO], recv_ocorner[0, 1], recv_ocorner[0, 0]),
        jnp.where(right, recv_opack[1], recv_opack[0]),
        jnp.where(right[0:OHALO], recv_ocorner[1, 1], recv_ocorner[1, 0]),
    ], axis=0)
    state = []
    for a in range(4):
        sides = pltpu.roll(side_rows, lanes - 16 * a, 1) if a else side_rows
        state.append(jnp.concatenate([oext[a, :, 0:ocols], sides], axis=1))
    surface, flux_strike, flux_dip, still = state

    row_at = lax.broadcasted_iota(jnp.int32, (all_rows, oext_cols), 0) + (sec * rows - OHALO)
    col = lax.broadcasted_iota(jnp.int32, (all_rows, oext_cols), 1)
    col_at = jnp.where(col < ocols + lanes // 2, col, col - oext_cols) + blk * ocols
    wet = ((row_at >= 0) & (row_at < n_sec * rows)) & ((col_at >= 0) & (col_at < n_blk * ocols))
    surface = jnp.where(wet, surface + source[...], 0.0)
    pull = wave_step * 0.5 * still
    for _ in range(WAVE_STEPS):
        change = (rows_up(flux_strike) - rows_down(flux_strike)) + (
            lanes_up(flux_dip) - lanes_down(flux_dip))
        surface = jnp.where(wet, surface - wave_step * 0.5 * change, 0.0)
        flux_strike = flux_strike - pull * (rows_up(surface) - rows_down(surface))
        flux_dip = flux_dip - pull * (lanes_up(surface) - lanes_down(surface))
    for a, value in enumerate((surface, flux_strike, flux_dip)):
        ocean_out[a] = value[OHALO:OHALO + rows, 0:ocols]

    for d in range(2):
        @pl.when(has_sec(SEC_DIRS[d]))
        def _():
            for i in range(3):
                sec_copy(d, i).wait_send()
            src_copy(d).wait_send()
        for e in range(2):
            @pl.when(both(d, e))
            def _():
                for i in range(3):
                    diag_copy(d, e, i).wait_send()
    for e in range(2):
        @pl.when(has_blk(SEC_DIRS[e]))
        def _():
            for i in range(3):
                blk_copy(e, i).wait_send()
    for turn in range(1, n_blk):
        up_copy(turn).wait_send()


def on_device(
    slab_state, buoyancy, lame_lambda, lame_mu, face_map, band_widths, ocean_state, water_depth
):
    n_blk = lax.axis_size("blk")
    thick, rows, lanes = slab_state.shape[1:]
    ocols = ocean_state.shape[2]
    dip = face_map.shape[0]
    ext_rows = rows + 8
    oext_cols = ocols + lanes
    f32 = jnp.float32
    vmem = pl.BlockSpec(memory_space=pltpu.VMEM)
    hbm = pl.BlockSpec(memory_space=pltpu.HBM)
    dma = pltpu.SemaphoreType.DMA
    return pl.pallas_call(
        kernel_body,
        out_shape=(
            jax.ShapeDtypeStruct(slab_state.shape, f32),
            jax.ShapeDtypeStruct(ocean_state.shape, f32),
        ),
        in_specs=[hbm] * 8,
        out_specs=(vmem, vmem),
        scratch_shapes=[
            pltpu.VMEM((ALL, thick + 2, ext_rows, 2 * lanes), f32),
            pltpu.VMEM((2, thick, ALL * HALO, lanes), f32),
            pltpu.VMEM((2, thick, ALL * HALO, lanes), f32),
            pltpu.VMEM((thick, rows, lanes), f32),
            pltpu.VMEM((2, thick, rows, lanes), f32),
            pltpu.VMEM((2, thick, HALO, lanes), f32),
            pltpu.VMEM((2, 2, thick, HALO, lanes), f32),
            pltpu.VMEM((thick, ext_rows, lanes), f32),
            pltpu.VMEM((4, rows + 2 * OHALO, oext_cols), f32),
            pltpu.VMEM((rows, lanes), f32),
            pltpu.VMEM((2, rows, lanes), f32),
            pltpu.VMEM((2, 2, OHALO, lanes), f32),
            pltpu.VMEM((1, dip), jnp.int32),
            pltpu.VMEM(band_widths.shape, jnp.int32),
            pltpu.VMEM((n_blk, rows, lanes), f32),
            pltpu.VMEM((rows + 2 * OHALO, oext_cols), f32),
            pltpu.VMEM((oext_cols, dip), jnp.bfloat16),
            pltpu.VMEM((oext_cols, dip), jnp.bfloat16),
            dma((8,)),
            dma((2, 3)), dma((2, 3)),
            dma((2, 3)), dma((2, 3)),
            dma((2, 2, 3)), dma((2, 2, 3)),
            dma((n_blk,)), dma((n_blk,)),
            dma((2,)), dma((2,)),
        ],
        compiler_params=pltpu.CompilerParams(
            collective_id=0, has_side_effects=True, vmem_limit_bytes=62 * 1024 * 1024
        ),
        cost_estimate=pl.CostEstimate(
            flops=200_000_000, bytes_accessed=2_000_000, transcendentals=500_000),
    )(
        slab_state, buoyancy, lame_lambda, lame_mu, face_map.reshape(1, dip), band_widths,
        ocean_state, water_depth,
    )


def solution(mesh):
    in_specs = (
        P(None, None, "sec", "blk"),
        P(None, "sec", "blk"),
        P(None, "sec", "blk"),
        P(None, "sec", "blk"),
        P(),
        P("sec", None),
        P(None, "sec", "blk"),
        P("sec", "blk"),
    )
    out_specs = (P(None, None, "sec", "blk"), P(None, "sec", "blk"))
    return jax.shard_map(
        on_device, mesh=mesh, in_specs=in_specs, out_specs=out_specs, check_vma=False
    )
```

time: 25 us -> 21.1 us (0.84)
  the two profiles are of different devices: /device:TPU:17 before, /device:TPU:0 now
where the time goes in v2:
time: 21.1 us; the launch traced here: 20.9 us
  Pallas kernels  17.7 us (84%)
  local copies, waits for them, and re-layouts  2.6 us (12%)
  between operations  0.65 us (3%)
    pallas_call x1, Pallas kernels, on_device(): pl.pallas_call(kernel_body, out_shape=(jax.ShapeDtypeStruct(slab_state.sh...  17.7 us
    unnamed x4, local copies, waits for them, and re-layouts  2.6 us

profile of v2, /device:TPU:0, one launch (start us, length us, event | category | flops | bytes accessed | tf_op | source)
XLA Modules:
  0.0 20.9 jit_solution(15071128255703262073)
XLA Ops:
  0.6 17.7 %shard_map.95 = (f32[9,8,16,128]{3,2,1,0:T(8,128)}, f32[3,16,512]{2,1,0:T(8,128)}) custom-call(f32[9,8,16,128]{3,2,1,0:T(8,128)} %slab.1, f32[8,16,128]{2,1,0:T(8,128)} %buoyancy.1, f32[8,16,128]{2,1,0:T(8,128)} %lame_lambda.1, f32[8,16,128]{2,1,0:T(8,128)} %lame_mu.1, s32[1,256]{1,0:T(1,128)} %bitcast.1, s32[1,2]{1,0:T(1,128)} %bands_hbm.1, ...), custom_call_target="tpu_custom_call" | custom-call | flops 200000000 | bytes 2000000 | tf_op jit(solution)/shard_map/pallas_call | solution.py:434
  18.3 0.0 copy-start
  18.3 2.0 %copy.12 = f32[9,8,16,128]{3,2,1,0:T(8,128)} copy(f32[9,8,16,128]{3,2,1,0:T(8,128)} %get-tuple-element.4) | data formatting | bytes 1179648
  20.3 0.0 copy-done
  20.3 0.6 %copy.13 = f32[3,16,512]{2,1,0:T(8,128)} copy(f32[3,16,512]{2,1,0:T(8,128)S(1)} %copy-done) | data formatting | bytes 196608
Async XLA Ops:
  18.3 2.0 %copy-start = (f32[3,16,512]{2,1,0:T(8,128)S(1)}, f32[3,16,512]{2,1,0:T(8,128)}, u32[]{:S(2)}) copy-start(f32[3,16,512]{2,1,0:T(8,128)} %get-tuple-element.5) | copy-start | bytes 294916

commit v3 on v2

--- a/solution.py
+++ b/solution.py
@@ -19,6 +19,27 @@
 HALO = 2
 OHALO = 8
 FRONT = 3
+
+TWO_ROWS = ((S12, S22, S23, V2, BUO), (S11, S12, S13, S22, S23, S33, V1, V3, BUO))
+ONE_ROW = ((S11, S13, S33, V1, V3, LAM, MU), (V2, LAM, MU))
+
+
+def per_layer(d):
+    return HALO * len(TWO_ROWS[d]) + len(ONE_ROW[d])
+
+
+def part_rows(d, layers):
+    return -(-per_layer(d) * layers // 8) * 8
+
+
+def row_pieces(d, t):
+    at = (t if t < FRONT else t - FRONT) * per_layer(d)
+    for f in TWO_ROWS[d]:
+        yield f, HALO, at
+        at += HALO
+    for f in ONE_ROW[d]:
+        yield f, 1, at
+        at += 1
 
 SEC_DIRS = (1, -1)
 
@@ -122,8 +143,8 @@
         if i == 2:
             src, dst = oext.at[:, out_rows, ocean_cols], oext.at[:, to_rows, ocean_cols]
         else:
-            part = (front, back)[i]
-            src, dst = send_rows.at[d, part], recv_rows.at[d, part]
+            part = pl.ds(0, part_rows(d, (FRONT, thick - FRONT)[i]))
+            src, dst = send_rows.at[d, i, part], recv_rows.at[d, i, part]
         return remote(src, dst, sec_send.at[d, i], sec_recv.at[d, i], (sec + SEC_DIRS[d], blk))
 
     def blk_copy(e, i):
@@ -185,10 +206,13 @@
         packed = jnp.zeros((rows, lanes), jnp.float32)
         for f in range(ALL):
             value = ext[f, t + 1, 0:rows, 0:lanes]
-            send_rows[0, t, HALO * f:HALO * f + HALO, :] = value[rows - HALO:, :]
-            send_rows[1, t, HALO * f:HALO * f + HALO, :] = value[0:HALO, :]
             moved = pltpu.roll(value, 4 * f, 1) if f else value
             packed = jnp.where(((lane - 4 * f + 2) & (lanes - 1)) < 4, moved, packed)
+        i = 0 if t < FRONT else 1
+        for f, count, at in row_pieces(0, t):
+            send_rows[0, i, at:at + count, :] = ext[f, t + 1, rows - count:rows, 0:lanes]
+        for f, count, at in row_pieces(1, t):
+            send_rows[1, i, at:at + count, :] = ext[f, t + 1, 0:count, 0:lanes]
         pack[t] = packed
         send_corner[0, t] = packed[rows - HALO:, :]
         send_corner[1, t] = packed[0:HALO, :]
@@ -255,10 +279,13 @@
         ext_pack[t, before, :] = jnp.where(few, recv_corner[0, 1, t], recv_corner[0, 0, t])
         sides = ext_pack[t]
         for f in range(ALL):
-            ext[f, t + 1, after, 0:lanes] = recv_rows[1, t, HALO * f:HALO * f + HALO, :]
-            ext[f, t + 1, before, 0:lanes] = recv_rows[0, t, HALO * f:HALO * f + HALO, :]
             ext[f, t + 1, :, lanes:2 * lanes] = (
                 pltpu.roll(sides, lanes - 4 * f, 1) if f else sides)
+        i = 0 if t < FRONT else 1
+        for f, count, at in row_pieces(0, t):
+            ext[f, t + 1, ext_rows - count:ext_rows, 0:lanes] = recv_rows[0, i, at:at + count, :]
+        for f, count, at in row_pieces(1, t):
+            ext[f, t + 1, rows:rows + count, 0:lanes] = recv_rows[1, i, at:at + count, :]
 
     def velocity_1(u, s11, s11_next, s12, s13):
         return ext[V1, u] + time_step * ext[BUO, u] * (
@@ -370,33 +397,19 @@
         def _():
             src_copy(d).wait_recv()
 
-    all_rows = rows + 2 * OHALO
     right = (lane & 15) < 8
     side_rows = jnp.concatenate([
         jnp.where(right[0:OHALO], recv_ocorner[0, 1], recv_ocorner[0, 0]),
         jnp.where(right, recv_opack[1], recv_opack[0]),
         jnp.where(right[0:OHALO], recv_ocorner[1, 1], recv_ocorner[1, 0]),
     ], axis=0)
-    state = []
     for a in range(4):
         sides = pltpu.roll(side_rows, lanes - 16 * a, 1) if a else side_rows
-        state.append(jnp.concatenate([oext[a, :, 0:ocols], sides], axis=1))
-    surface, flux_strike, flux_dip, still = state
-
-    row_at = lax.broadcasted_iota(jnp.int32, (all_rows, oext_cols), 0) + (sec * rows - OHALO)
-    col = lax.broadcasted_iota(jnp.int32, (all_rows, oext_cols), 1)
-    col_at = jnp.where(col < ocols + lanes // 2, col, col - oext_cols) + blk * ocols
-    wet = ((row_at >= 0) & (row_at < n_sec * rows)) & ((col_at >= 0) & (col_at < n_blk * ocols))
-    surface = jnp.where(wet, surface + source[...], 0.0)
-    pull = wave_step * 0.5 * still
-    for _ in range(WAVE_STEPS):
-        change = (rows_up(flux_strike) - rows_down(flux_strike)) + (
-            lanes_up(flux_dip) - lanes_down(flux_dip))
-        surface = jnp.where(wet, surface - wave_step * 0.5 * change, 0.0)
-        flux_strike = flux_strike - pull * (rows_up(surface) - rows_down(surface))
-        flux_dip = flux_dip - pull * (lanes_up(surface) - lanes_down(surface))
-    for a, value in enumerate((surface, flux_strike, flux_dip)):
-        ocean_out[a] = value[OHALO:OHALO + rows, 0:ocols]
+        own = oext[a, :, 0:ocols]
+        if a == 0:
+            own, sides = own + source[:, 0:ocols], sides + source[:, ocols:]
+        ocean_out[a, :, 0:ocols] = own
+        ocean_out[a, :, ocols:] = sides
 
     for d in range(2):
         @pl.when(has_sec(SEC_DIRS[d]))
@@ -418,6 +431,36 @@
         up_copy(turn).wait_send()
 
 
+def wave_body(slab, state, slab_out, ocean_out, result, slab_sem, ocean_sem):
+    n_sec = lax.axis_size("sec")
+    n_blk = lax.axis_size("blk")
+    sec = lax.axis_index("sec")
+    blk = lax.axis_index("blk")
+    rows, ocols = result.shape[1:]
+    all_rows, oext_cols = state.shape[1:]
+    slab_copy = pltpu.make_async_copy(slab, slab_out, slab_sem)
+    slab_copy.start()
+    surface, flux_strike, flux_dip, still = (state[a] for a in range(4))
+    row_at = lax.broadcasted_iota(jnp.int32, (all_rows, oext_cols), 0) + (sec * rows - OHALO)
+    col = lax.broadcasted_iota(jnp.int32, (all_rows, oext_cols), 1)
+    col_at = jnp.where(col < (ocols + oext_cols) // 2, col, col - oext_cols) + blk * ocols
+    wet = ((row_at >= 0) & (row_at < n_sec * rows)) & ((col_at >= 0) & (col_at < n_blk * ocols))
+    surface = jnp.where(wet, surface, 0.0)
+    pull = wave_step * 0.5 * still
+    for _ in range(WAVE_STEPS):
+        change = (rows_up(flux_strike) - rows_down(flux_strike)) + (
+            lanes_up(flux_dip) - lanes_down(flux_dip))
+        surface = jnp.where(wet, surface - wave_step * 0.5 * change, 0.0)
+        flux_strike = flux_strike - pull * (rows_up(surface) - rows_down(surface))
+        flux_dip = flux_dip - pull * (lanes_up(surface) - lanes_down(surface))
+    for a, value in enumerate((surface, flux_strike, flux_dip)):
+        result[a] = value[OHALO:OHALO + rows, 0:ocols]
+    ocean_copy = pltpu.make_async_copy(result, ocean_out, ocean_sem)
+    ocean_copy.start()
+    slab_copy.wait()
+    ocean_copy.wait()
+
+
 def on_device(
     slab_state, buoyancy, lame_lambda, lame_mu, face_map, band_widths, ocean_state, water_depth
 ):
@@ -427,22 +470,23 @@
     dip = face_map.shape[0]
     ext_rows = rows + 8
     oext_cols = ocols + lanes
+    max_rows = max(part_rows(d, n) for d in range(2) for n in (FRONT, thick - FRONT))
     f32 = jnp.float32
     vmem = pl.BlockSpec(memory_space=pltpu.VMEM)
     hbm = pl.BlockSpec(memory_space=pltpu.HBM)
     dma = pltpu.SemaphoreType.DMA
-    return pl.pallas_call(
+    slab_done, state = pl.pallas_call(
         kernel_body,
         out_shape=(
             jax.ShapeDtypeStruct(slab_state.shape, f32),
-            jax.ShapeDtypeStruct(ocean_state.shape, f32),
+            jax.ShapeDtypeStruct((4, rows + 2 * OHALO, oext_cols), f32),
         ),
         in_specs=[hbm] * 8,
         out_specs=(vmem, vmem),
         scratch_shapes=[
             pltpu.VMEM((ALL, thick + 2, ext_rows, 2 * lanes), f32),
-            pltpu.VMEM((2, thick, ALL * HALO, lanes), f32),
-            pltpu.VMEM((2, thick, ALL * HALO, lanes), f32),
+            pltpu.VMEM((2, 2, max_rows, lanes), f32),
+            pltpu.VMEM((2, 2, max_rows, lanes), f32),
             pltpu.VMEM((thick, rows, lanes), f32),
             pltpu.VMEM((2, thick, rows, lanes), f32),
             pltpu.VMEM((2, thick, HALO, lanes), f32),
@@ -466,14 +510,26 @@
             dma((2,)), dma((2,)),
         ],
         compiler_params=pltpu.CompilerParams(
-            collective_id=0, has_side_effects=True, vmem_limit_bytes=62 * 1024 * 1024
+            collective_id=0, has_side_effects=True, vmem_limit_bytes=32 * 1024 * 1024
         ),
         cost_estimate=pl.CostEstimate(
             flops=200_000_000, bytes_accessed=2_000_000, transcendentals=500_000),
     )(
-        slab_state, buoyancy, lame_lambda, lame_mu, face_map.reshape(1, dip), band_widths,
-        ocean_state, water_depth,
+        *(pltpu.with_memory_space_constraint(x, pltpu.HBM) for x in (
+            slab_state, buoyancy, lame_lambda, lame_mu, face_map.reshape(1, dip), band_widths,
+            ocean_state, water_depth))
     )
+    return pl.pallas_call(
+        wave_body,
+        out_shape=(
+            jax.ShapeDtypeStruct(slab_state.shape, f32),
+            jax.ShapeDtypeStruct(ocean_state.shape, f32),
+        ),
+        in_specs=[pl.BlockSpec(memory_space=pl.ANY), vmem],
+        out_specs=(hbm, hbm),
+        scratch_shapes=[pltpu.VMEM(ocean_state.shape, f32), dma, dma],
+        compiler_params=pltpu.CompilerParams(vmem_limit_bytes=16 * 1024 * 1024),
+    )(slab_done, state)
 
 
 def solution(mesh):

time: 21.1 us -> 17.8 us (0.84)
  local copies, waits for them, and re-layouts: 2.6 us -> 0 us
  Pallas kernels: 17.7 us -> 17 us
    unnamed x4 -> x0, local copies, waits for them, and re-layouts: 2.6 us -> none
    pallas_call x1, Pallas kernels: 17.7 us -> 15.4 us  [on_device(): pl.pallas_call(kernel_body, out_shape=(jax.ShapeDtypeStruct(slab_state.sh...]
    pallas_call x0 -> x1, Pallas kernels: none -> 1.54 us  [on_device(): pl.pallas_call(wave_body, out_shape=(jax.ShapeDtypeStruct(slab_state.shap...]
where the time goes in v3:
time: 17.8 us; the launch traced here: 17.6 us
  Pallas kernels  17 us (96%)
  between operations  0.64 us (4%)
    pallas_call x1, Pallas kernels, on_device(): pl.pallas_call(kernel_body, out_shape=(jax.ShapeDtypeStruct(slab_state.sh...  15.4 us
    pallas_call x1, Pallas kernels, on_device(): pl.pallas_call(wave_body, out_shape=(jax.ShapeDtypeStruct(slab_state.shap...  1.54 us

profile of v3, /device:TPU:0, one launch (start us, length us, event | category | flops | bytes accessed | tf_op | source)
XLA Modules:
  0.0 17.6 jit_solution(6313277168519483616)
XLA Ops:
  0.6 15.4 %shard_map.95 = (f32[9,8,16,128]{3,2,1,0:T(8,128)S(1)}, f32[4,32,640]{2,1,0:T(8,128)S(1)}) custom-call(f32[9,8,16,128]{3,2,1,0:T(8,128)} %slab.1, f32[8,16,128]{2,1,0:T(8,128)} %buoyancy.1, f32[8,16,128]{2,1,0:T(8,128)} %lame_lambda.1, f32[8,16,128]{2,1,0:T(8,128)} %lame_mu.1, s32[1,256]{1,0:T(1,128)} %bitcast.1, s32[1,2]{1,0:T(1,128)} %bands_hbm.1, ...), custom_call_target="tpu_custom_call" | custom-call | flops 200000000 | bytes 2000000 | tf_op jit(solution)/shard_map/pallas_call | solution.py:478
  16.1 1.5 %shard_map.96 = (f32[9,8,16,128]{3,2,1,0:T(8,128)}, f32[3,16,512]{2,1,0:T(8,128)}) custom-call(f32[9,8,16,128]{3,2,1,0:T(8,128)S(1)} %get-tuple-element.4.slab, f32[4,32,640]{2,1,0:T(8,128)S(1)} %get-tuple-element.5.state), custom_call_target="tpu_custom_call" | custom-call | tf_op jit(solution)/shard_map/pallas_call | solution.py:522

commit v4 on v3

--- a/solution.py
+++ b/solution.py
@@ -64,7 +64,7 @@
     slab, buoyancy, lame_lambda, lame_mu, face_hbm, bands_hbm, ocean, depth,
     slab_out, ocean_out,
     ext, send_rows, recv_rows, pack, recv_pack, send_corner, recv_corner, ext_pack,
-    oext, opack, recv_opack, recv_ocorner, face_map, bands, uplift, source, k_hi, k_lo,
+    oext, opack, recv_opack, recv_ocorner, face_map, bands, uplift, level, k_hi, k_lo,
     load_sem, sec_send, sec_recv, blk_send, blk_recv, diag_send, diag_recv,
     up_send, up_recv, src_send, src_recv,
 ):
@@ -109,7 +109,7 @@
     recv_opack[...] = jnp.zeros_like(recv_opack)
     recv_ocorner[...] = jnp.zeros_like(recv_ocorner)
     for first in (0, OHALO + rows):
-        source[first:first + OHALO, :] = jnp.zeros((OHALO, oext_cols), jnp.float32)
+        level[first:first + OHALO, :] = jnp.zeros((OHALO, oext_cols), jnp.float32)
         oext[:, first:first + OHALO, 0:ocols] = jnp.zeros((4, OHALO, ocols), jnp.float32)
 
     barrier = pltpu.get_barrier_semaphore()
@@ -141,7 +141,8 @@
         out_rows = pl.ds(rows, OHALO) if d == 0 else pl.ds(OHALO, OHALO)
         to_rows = pl.ds(0, OHALO) if d == 0 else pl.ds(OHALO + rows, OHALO)
         if i == 2:
-            src, dst = oext.at[:, out_rows, ocean_cols], oext.at[:, to_rows, ocean_cols]
+            fluxes = pl.ds(1, 3)
+            src, dst = oext.at[fluxes, out_rows, ocean_cols], oext.at[fluxes, to_rows, ocean_cols]
         else:
             part = pl.ds(0, part_rows(d, (FRONT, thick - FRONT)[i]))
             src, dst = send_rows.at[d, i, part], recv_rows.at[d, i, part]
@@ -356,14 +357,10 @@
     for turn in range(1, n_blk):
         up_copy(turn).start()
 
-    await_all(1)
-    for t in range(FRONT, thick):
-        assemble(t)
-    for t in range(2, thick):
-        velocity(t)
-    for t in range(1, thick):
-        stress(t)
-
+    for e in range(2):
+        @pl.when(has_blk(-SEC_DIRS[e]))
+        def _():
+            blk_copy(e, 2).wait_recv()
     for turn in range(1, n_blk):
         up_arrival(turn).wait_recv()
     whole = jnp.concatenate([uplift[b] for b in range(n_blk)], axis=1)
@@ -373,43 +370,58 @@
     by_high = lax.dot_general(jnp.concatenate([high, low], axis=0), k_hi[...], dims,
                               preferred_element_type=jnp.float32)
     by_low = lax.dot_general(high, k_lo[...], dims, preferred_element_type=jnp.float32)
-    source[OHALO:OHALO + rows, :] = by_high[0:rows] + (by_high[rows:] + by_low)
+    own_source = by_high[0:rows] + (by_high[rows:] + by_low)
+    right = (lane & 15) < 8
+    beside = jnp.where(right, recv_opack[1], recv_opack[0])
+    level[OHALO:OHALO + rows, 0:ocols] = oext[0, ocean_rows, ocean_cols] + own_source[:, 0:ocols]
+    level[OHALO:OHALO + rows, ocols:] = beside + own_source[:, ocols:]
 
     def src_copy(d):
         out_rows = pl.ds(rows, OHALO) if d == 0 else pl.ds(OHALO, OHALO)
         to_rows = pl.ds(0, OHALO) if d == 0 else pl.ds(OHALO + rows, OHALO)
-        return remote(source.at[out_rows], source.at[to_rows], src_send.at[d], src_recv.at[d],
+        return remote(level.at[out_rows], level.at[to_rows], src_send.at[d], src_recv.at[d],
                       (sec + SEC_DIRS[d], blk))
 
     for d in range(2):
         @pl.when(has_sec(SEC_DIRS[d]))
         def _():
             src_copy(d).start()
+
+    await_all(1)
+    for t in range(FRONT, thick):
+        assemble(t)
+    for t in range(2, thick):
+        velocity(t)
+    for t in range(1, thick):
+        stress(t)
 
     for t in range(thick):
         velocity(t)
     for t in range(thick):
         last_stress(t)
 
-    await_all(2)
     for d in range(2):
         @pl.when(has_sec(-SEC_DIRS[d]))
         def _():
+            sec_copy(d, 2).wait_recv()
+        for e in range(2):
+            @pl.when(from_both(d, e))
+            def _():
+                diag_copy(d, e, 2).wait_recv()
+    for d in range(2):
+        @pl.when(has_sec(-SEC_DIRS[d]))
+        def _():
             src_copy(d).wait_recv()
 
-    right = (lane & 15) < 8
     side_rows = jnp.concatenate([
         jnp.where(right[0:OHALO], recv_ocorner[0, 1], recv_ocorner[0, 0]),
-        jnp.where(right, recv_opack[1], recv_opack[0]),
+        beside,
         jnp.where(right[0:OHALO], recv_ocorner[1, 1], recv_ocorner[1, 0]),
     ], axis=0)
-    for a in range(4):
-        sides = pltpu.roll(side_rows, lanes - 16 * a, 1) if a else side_rows
-        own = oext[a, :, 0:ocols]
-        if a == 0:
-            own, sides = own + source[:, 0:ocols], sides + source[:, ocols:]
-        ocean_out[a, :, 0:ocols] = own
-        ocean_out[a, :, ocols:] = sides
+    ocean_out[0] = level[...]
+    for a in range(1, 4):
+        ocean_out[a, :, 0:ocols] = oext[a, :, 0:ocols]
+        ocean_out[a, :, ocols:] = pltpu.roll(side_rows, lanes - 16 * a, 1)
 
     for d in range(2):
         @pl.when(has_sec(SEC_DIRS[d]))

time: 17.8 us -> 16.1 us (0.904)
  the two profiles are of different devices: /device:TPU:0 before, /device:TPU:8 now
where the time goes in v4:
time: 16.1 us; the launch traced here: 15.9 us
  Pallas kernels  15.3 us (95%)
  between operations  0.64 us (4%)
    pallas_call x1, Pallas kernels, on_device(): pl.pallas_call(kernel_body, out_shape=(jax.ShapeDtypeStruct(slab_state.sh...  13.7 us
    pallas_call x1, Pallas kernels, on_device(): pl.pallas_call(wave_body, out_shape=(jax.ShapeDtypeStruct(slab_state.shap...  1.54 us

profile of v4, /device:TPU:8, one launch (start us, length us, event | category | flops | bytes accessed | tf_op | source)
XLA Modules:
  0.0 15.9 jit_solution(3263761811376379751)
XLA Ops:
  0.6 13.7 %shard_map.95 = (f32[9,8,16,128]{3,2,1,0:T(8,128)S(1)}, f32[4,32,640]{2,1,0:T(8,128)S(1)}) custom-call(f32[9,8,16,128]{3,2,1,0:T(8,128)} %slab.1, f32[8,16,128]{2,1,0:T(8,128)} %buoyancy.1, f32[8,16,128]{2,1,0:T(8,128)} %lame_lambda.1, f32[8,16,128]{2,1,0:T(8,128)} %lame_mu.1, s32[1,256]{1,0:T(1,128)} %bitcast.1, s32[1,2]{1,0:T(1,128)} %bands_hbm.1, ...), custom_call_target="tpu_custom_call" | custom-call | flops 200000000 | bytes 2000000 | tf_op jit(solution)/shard_map/pallas_call | solution.py:490
  14.4 1.5 %shard_map.96 = (f32[9,8,16,128]{3,2,1,0:T(8,128)}, f32[3,16,512]{2,1,0:T(8,128)}) custom-call(f32[9,8,16,128]{3,2,1,0:T(8,128)S(1)} %get-tuple-element.4.slab, f32[4,32,640]{2,1,0:T(8,128)S(1)} %get-tuple-element.5.state), custom_call_target="tpu_custom_call" | custom-call | tf_op jit(solution)/shard_map/pallas_call | solution.py:534

commit v5 on v4

--- a/solution.py
+++ b/solution.py
@@ -246,26 +246,31 @@
             total = jnp.where(blk + step == j, bands[0:1, j:j + 1].astype(jnp.float32), total)
         return jnp.maximum(total, 1.0)
 
-    chunk = 32
+    chunk = 64
     face = face_map[...].astype(jnp.float32)
     index = lax.broadcasted_iota(jnp.int32, (chunk, dip), 0).astype(jnp.float32)
     own_column = (blk * ocols).astype(jnp.float32)
 
     def fill(first, column, count, width):
-        distance = jnp.abs((index[0:count] + (own_column + float(column))) - face)
+        distance = jnp.abs((index[0:count] + column) - face)
         decay = jnp.exp2(distance * (-math.pi / 2.0 * math.log2(math.e) / width))
         under = width + width * (decay * decay)
         guess = pl.reciprocal(under, approx=True)
         value = decay * (guess * (2.0 - under * guess))
         high = value.astype(jnp.bfloat16)
-        k_hi[first:first + count, :] = high
-        k_lo[first:first + count, :] = (value - high.astype(jnp.float32)).astype(jnp.bfloat16)
+        k_hi[pl.ds(first, count), :] = high
+        k_lo[pl.ds(first, count), :] = (value - high.astype(jnp.float32)).astype(jnp.bfloat16)
 
     here = width_at(0)
-    for first in range(0, ocols, chunk):
-        fill(first, first, chunk, here)
-    fill(ocols, ocols, 16, width_at(1))
-    fill(oext_cols - 16, -16, 16, width_at(-1))
+
+    def fill_chunk(i, carry):
+        first = pl.multiple_of(i * chunk, chunk)
+        fill(first, own_column + first.astype(jnp.float32), chunk, here)
+        return carry
+
+    lax.fori_loop(0, ocols // chunk, fill_chunk, 0)
+    fill(ocols, own_column + float(ocols), 16, width_at(1))
+    fill(oext_cols - 16, own_column - 16.0, 16, width_at(-1))
     blank = jnp.zeros((oext_cols - ocols - 32, dip), jnp.bfloat16)
     k_hi[ocols + 16:oext_cols - 16, :] = blank
     k_lo[ocols + 16:oext_cols - 16, :] = blank
@@ -332,6 +337,14 @@
         for f, value in stress_values(t + 1):
             slab_out[f, t] = value[0:rows, 0:lanes]
 
+    def layers_in_turn(first, end, step):
+        def two(i, carry):
+            step(first + 2 * i)
+            step(first + 2 * i + 1)
+            return carry
+
+        lax.fori_loop(0, (end - first) // 2, two, 0)
+
     await_all(0)
     for t in range(FRONT):
         assemble(t)
@@ -390,15 +403,12 @@
     await_all(1)
     for t in range(FRONT, thick):
         assemble(t)
-    for t in range(2, thick):
-        velocity(t)
-    for t in range(1, thick):
-        stress(t)
-
-    for t in range(thick):
-        velocity(t)
-    for t in range(thick):
-        last_stress(t)
+    layers_in_turn(2, thick, velocity)
+    stress(1)
+    layers_in_turn(2, thick, stress)
+
+    layers_in_turn(0, thick, velocity)
+    layers_in_turn(0, thick, last_stress)
 
     for d in range(2):
         @pl.when(has_sec(-SEC_DIRS[d]))

time: 16.1 us -> 16.1 us (level)
  no operation moved by 1% of the time
where the time goes in v5:
time: 16.1 us; the launch traced here: 15.9 us
  Pallas kernels  15.3 us (95%)
  between operations  0.64 us (4%)
    pallas_call x1, Pallas kernels, on_device(): pl.pallas_call(kernel_body, out_shape=(jax.ShapeDtypeStruct(slab_state.sh...  13.7 us
    pallas_call x1, Pallas kernels, on_device(): pl.pallas_call(wave_body, out_shape=(jax.ShapeDtypeStruct(slab_state.shap...  1.54 us

profile of v5, /device:TPU:8, one launch (start us, length us, event | category | flops | bytes accessed | tf_op | source)
XLA Modules:
  0.0 15.9 jit_solution(5175014305172764533)
XLA Ops:
  0.6 13.7 %shard_map.95 = (f32[9,8,16,128]{3,2,1,0:T(8,128)S(1)}, f32[4,32,640]{2,1,0:T(8,128)S(1)}) custom-call(f32[9,8,16,128]{3,2,1,0:T(8,128)} %slab.1, f32[8,16,128]{2,1,0:T(8,128)} %buoyancy.1, f32[8,16,128]{2,1,0:T(8,128)} %lame_lambda.1, f32[8,16,128]{2,1,0:T(8,128)} %lame_mu.1, s32[1,256]{1,0:T(1,128)} %bitcast.1, s32[1,2]{1,0:T(1,128)} %bands_hbm.1, ...), custom_call_target="tpu_custom_call" | custom-call | flops 200000000 | bytes 2000000 | tf_op jit(solution)/shard_map/pallas_call | solution.py:500
  14.4 1.5 %shard_map.96 = (f32[9,8,16,128]{3,2,1,0:T(8,128)}, f32[3,16,512]{2,1,0:T(8,128)}) custom-call(f32[9,8,16,128]{3,2,1,0:T(8,128)S(1)} %get-tuple-element.4.slab, f32[4,32,640]{2,1,0:T(8,128)S(1)} %get-tuple-element.5.state), custom_call_target="tpu_custom_call" | custom-call | tf_op jit(solution)/shard_map/pallas_call | solution.py:544

commit v6 on v4

--- a/solution.py
+++ b/solution.py
@@ -88,12 +88,15 @@
 
     own_rows, own_lanes = pl.ds(0, rows), pl.ds(0, lanes)
     ocean_rows, ocean_cols = pl.ds(OHALO, rows), pl.ds(0, ocols)
-    layers = pl.ds(1, thick)
-    loads = [
-        (slab, ext.at[pl.ds(0, FIELDS), layers, own_rows, own_lanes]),
-        (buoyancy, ext.at[BUO, layers, own_rows, own_lanes]),
-        (lame_lambda, ext.at[LAM, layers, own_rows, own_lanes]),
-        (lame_mu, ext.at[MU, layers, own_rows, own_lanes]),
+    loads = []
+    for part, layers in ((front, pl.ds(1, FRONT)), (back, pl.ds(1 + FRONT, thick - FRONT))):
+        loads += [
+            (slab.at[:, part], ext.at[pl.ds(0, FIELDS), layers, own_rows, own_lanes]),
+            (buoyancy.at[part], ext.at[BUO, layers, own_rows, own_lanes]),
+            (lame_lambda.at[part], ext.at[LAM, layers, own_rows, own_lanes]),
+            (lame_mu.at[part], ext.at[MU, layers, own_rows, own_lanes]),
+        ]
+    loads += [
         (face_hbm, face_map),
         (bands_hbm, bands),
         (ocean, oext.at[pl.ds(0, 3), ocean_rows, ocean_cols]),
@@ -225,11 +228,13 @@
     near = (n_blk - 1) + sum(jnp.where(has_sec(step), n_blk, 0) for step in SEC_DIRS)
     pl.semaphore_wait(barrier, near)
     send_all(0)
+    for load in loads[4:8]:
+        load.wait()
     for t in range(FRONT, thick):
         pack_layer(t)
     send_all(1)
 
-    for load in loads[4:]:
+    for load in loads[8:]:
         load.wait()
     opacked = jnp.zeros((rows, lanes), jnp.float32)
     for a in range(4):
@@ -514,7 +519,7 @@
             pltpu.VMEM((rows + 2 * OHALO, oext_cols), f32),
             pltpu.VMEM((oext_cols, dip), jnp.bfloat16),
             pltpu.VMEM((oext_cols, dip), jnp.bfloat16),
-            dma((8,)),
+            dma((12,)),
             dma((2, 3)), dma((2, 3)),
             dma((2, 3)), dma((2, 3)),
             dma((2, 2, 3)), dma((2, 2, 3)),

time: 16.1 us -> 16.1 us (level)
  no operation moved by 1% of the time
where the time goes in v6:
time: 16.1 us; the launch traced here: 16 us
  Pallas kernels  15.3 us (95%)
  between operations  0.64 us (4%)
    pallas_call x1, Pallas kernels, on_device(): pl.pallas_call(kernel_body, out_shape=(jax.ShapeDtypeStruct(slab_state.sh...  13.8 us
    pallas_call x1, Pallas kernels, on_device(): pl.pallas_call(wave_body, out_shape=(jax.ShapeDtypeStruct(slab_state.shap...  1.54 us

profile of v6, /device:TPU:8, one launch (start us, length us, event | category | flops | bytes accessed | tf_op | source)
XLA Modules:
  0.0 16.0 jit_solution(14824462111796715917)
XLA Ops:
  0.6 13.8 %shard_map.95 = (f32[9,8,16,128]{3,2,1,0:T(8,128)S(1)}, f32[4,32,640]{2,1,0:T(8,128)S(1)}) custom-call(f32[9,8,16,128]{3,2,1,0:T(8,128)} %slab.1, f32[8,16,128]{2,1,0:T(8,128)} %buoyancy.1, f32[8,16,128]{2,1,0:T(8,128)} %lame_lambda.1, f32[8,16,128]{2,1,0:T(8,128)} %lame_mu.1, s32[1,256]{1,0:T(1,128)} %bitcast.1, s32[1,2]{1,0:T(1,128)} %bands_hbm.1, ...), custom_call_target="tpu_custom_call" | custom-call | flops 200000000 | bytes 2000000 | tf_op jit(solution)/shard_map/pallas_call | solution.py:495
  14.4 1.5 %shard_map.96 = (f32[9,8,16,128]{3,2,1,0:T(8,128)}, f32[3,16,512]{2,1,0:T(8,128)}) custom-call(f32[9,8,16,128]{3,2,1,0:T(8,128)S(1)} %get-tuple-element.4.slab, f32[4,32,640]{2,1,0:T(8,128)S(1)} %get-tuple-element.5.state), custom_call_target="tpu_custom_call" | custom-call | tf_op jit(solution)/shard_map/pallas_call | solution.py:539
